TPU v7x, 256 devices: a whole 4x4x8 slice. The times are simulated.
256 devices in a mesh: wide: 32 (over y, z), narrow: 8 (over x, core).
Axes of the slice: x: 4, y: 4, z: 8, core: 2. Of those that a mesh axis runs over, the one named last changes fastest.
Arguments:
- coefficients: float32 [3, 512, 64, 512], P(None, 'wide', 'narrow'), may hold values from 0.3 to 3
- predicted_velocity: float32 [3, 512, 64, 512], P(None, 'wide', 'narrow'), may hold values from -3 to 3
- tracers: float32 [16, 512, 64, 512], P(None, 'wide', 'narrow'), may hold values from 0.1 to 2
Outputs:
- pressure: float32 [512, 64, 512], P('wide', 'narrow')
- velocity: float32 [3, 512, 64, 512], P(None, 'wide', 'narrow')
- transported: float32 [16, 512, 64, 512], P(None, 'wide', 'narrow')
All inputs are finite; a program needn't handle non-finite values.
Results may differ from a plain program's by a relative error of at most 0.0001.
Values sent between devices are 32-bit elements; how exact they have to be, the bound alone decides.
A program may use at most 192 MiB of HBM per device.

v0:
```python
import jax
import jax.numpy as jnp
from jax import lax
from jax.sharding import PartitionSpec as P

ITERS = 3
SUBSTEPS = 2


COURANT = 0.15


def with_halo(block, sides, width):
    for axis, dim in sides:
        count = lax.axis_size(axis)
        forward = [(i, i + 1) for i in range(count - 1)]
        backward = [(target, source) for source, target in forward]
        low = lax.ppermute(
            lax.slice_in_dim(block, block.shape[dim] - width, None, axis=dim), axis, forward
        )
        high = lax.ppermute(lax.slice_in_dim(block, 0, width, axis=dim), axis, backward)
        block = jnp.concatenate([low, block, high], axis=dim)
    return block


def shifted(value, axis, by):
    devices = lax.axis_size(axis)
    pairs = [(i, i + by) for i in range(devices) if 0 <= i + by < devices]
    return lax.ppermute(value, axis, pairs)


def lower_local(field, axis, edge):
    rest = lax.slice_in_dim(field, 0, field.shape[axis] - 1, axis=axis)
    return jnp.concatenate([edge, rest], axis=axis)


def upwind_step(tracer_ext, flow_ext):
    span_a = tracer_ext.shape[1] - 2
    span_b = tracer_ext.shape[2] - 2
    inner = tracer_ext[:, 1 : span_a + 1, 1 : span_b + 1]
    speed = flow_ext[0, 0 : span_a + 1, 1 : span_b + 1]
    flux = (
        jnp.maximum(speed, 0.0) * tracer_ext[:, 0 : span_a + 1, 1 : span_b + 1]
        + jnp.minimum(speed, 0.0) * tracer_ext[:, 1 : span_a + 2, 1 : span_b + 1]
    )
    change = flux[:, 1:] - flux[:, :-1]
    speed = flow_ext[1, 1 : span_a + 1, 0 : span_b + 1]
    flux = (
        jnp.maximum(speed, 0.0) * tracer_ext[:, 1 : span_a + 1, 0 : span_b + 1]
        + jnp.minimum(speed, 0.0) * tracer_ext[:, 1 : span_a + 1, 1 : span_b + 2]
    )
    change = change + (flux[:, :, 1:] - flux[:, :, :-1])
    speed = flow_ext[2, 1 : span_a + 1, 1 : span_b + 1]
    above = jnp.concatenate([inner[..., 1:], jnp.zeros_like(inner[..., :1])], axis=3)
    flux = jnp.maximum(speed, 0.0) * inner + jnp.minimum(speed, 0.0) * above
    below = jnp.concatenate([jnp.zeros_like(flux[..., :1]), flux[..., :-1]], axis=3)
    change = change + (flux - below)
    return inner - COURANT * change


def pressure_flux(field, coefficients, beta_low_x, beta_low_y):
    padded = with_halo(field, (("wide", 0), ("narrow", 1)), 1)
    center = padded[1:-1, 1:-1]
    beta_x = jnp.concatenate([beta_low_x, coefficients[0]], axis=0)
    flux_x = beta_x * (padded[1:, 1:-1] - padded[:-1, 1:-1])
    beta_y = jnp.concatenate([beta_low_y, coefficients[1]], axis=1)
    flux_y = beta_y * (padded[1:-1, 1:] - padded[1:-1, :-1])
    above = jnp.concatenate([center[..., 1:], jnp.zeros_like(center[..., :1])], axis=2)
    flux_z = coefficients[2] * (above - center)
    return (flux_x, flux_y, flux_z)


def apply_operator(field, coefficients, beta_low_x, beta_low_y):
    flux_x, flux_y, flux_z = pressure_flux(field, coefficients, beta_low_x, beta_low_y)
    below = jnp.concatenate([jnp.zeros_like(flux_z[..., :1]), flux_z[..., :-1]], axis=2)
    return -(flux_x[1:] - flux_x[:-1] + (flux_y[:, 1:] - flux_y[:, :-1]) + (flux_z - below))


def precond_norm(residual, precond):
    return lax.psum(jnp.sum(residual * precond), ("wide", "narrow"))


def body(coefficients, predicted_velocity, tracers):
    beta_low_x, speed_low_x = shifted((coefficients[0, -1:], predicted_velocity[0, -1:]), "wide", 1)
    beta_low_y, speed_low_y = shifted(
        (coefficients[1, :, -1:], predicted_velocity[1, :, -1:]), "narrow", 1
    )
    zero_z = jnp.zeros_like(coefficients[2][..., :1])
    rhs = -(
        predicted_velocity[0]
        - lower_local(predicted_velocity[0], 0, speed_low_x)
        + (predicted_velocity[1] - lower_local(predicted_velocity[1], 1, speed_low_y))
        + (predicted_velocity[2] - lower_local(predicted_velocity[2], 2, zero_z))
    )
    diag = (
        coefficients[0]
        + lower_local(coefficients[0], 0, beta_low_x)
        + (coefficients[1] + lower_local(coefficients[1], 1, beta_low_y))
        + (coefficients[2] + lower_local(coefficients[2], 2, zero_z))
    )
    pressure = jnp.zeros_like(rhs)
    residual = rhs
    precond = residual / diag
    direction = precond
    inner = precond_norm(residual, precond)
    for step in range(ITERS):
        image = apply_operator(direction, coefficients, beta_low_x, beta_low_y)
        alpha = inner / lax.psum(jnp.sum(direction * image), ("wide", "narrow"))
        pressure = pressure + alpha * direction
        if step + 1 < ITERS:
            residual = residual - alpha * image
            precond = residual / diag
            inner_next = precond_norm(residual, precond)
            direction = precond + inner_next / inner * direction
            inner = inner_next
    flux_x, flux_y, flux_z = pressure_flux(pressure, coefficients, beta_low_x, beta_low_y)
    velocity = predicted_velocity - jnp.stack([flux_x[1:], flux_y[:, 1:], flux_z])
    speed_x_low = speed_low_x - flux_x[:1]
    speed_y_low = speed_low_y - flux_y[:, :1]
    ext_x = jnp.pad(jnp.concatenate([speed_x_low, velocity[0]], axis=0), ((0, 1), (1, 1), (0, 0)))
    ext_y = jnp.pad(jnp.concatenate([speed_y_low, velocity[1]], axis=1), ((1, 1), (0, 1), (0, 0)))
    ext_z = jnp.pad(velocity[2], ((1, 1), (1, 1), (0, 0)))
    flow_ext = jnp.stack([ext_x, ext_y, ext_z])
    current = tracers
    for sub in range(SUBSTEPS):
        padded = with_halo(current, (("wide", 1), ("narrow", 2)), 1)
        current = upwind_step(padded, flow_ext)
    return (pressure, velocity, current)


def solution(mesh):
    placed = (
        P(None, "wide", "narrow", None),
        P(None, "wide", "narrow", None),
        P(None, "wide", "narrow", None),
    )
    return jax.shard_map(
        body,
        mesh=mesh,
        in_specs=placed,
        out_specs=(
            P("wide", "narrow", None),
            P(None, "wide", "narrow", None),
            P(None, "wide", "narrow", None),
        ),
        check_vma=False,
    )
```

profile of v0, /device:TPU:1, one launch (start us, length us, event | category | flops | bytes accessed | tf_op | source)
XLA Modules:
  0.0 562.9 jit_solution(8185855109437586945)
XLA Ops:
  1.6 4.5 collective-permute-start.3
  6.9 3.5 collective-permute-start.2
  11.4 2.2 collective-permute-start.1
  14.3 3.7 collective-permute-start
  18.0 5.4 copy.13
  24.3 4.3 collective-permute-start.20
  30.7 4.7 collective-permute-start.5
  36.3 3.5 collective-permute-start.6
  39.8 3.0 collective-permute-start.7
  44.9 78.4 %all-reduce.16 = (f32[]{:T(128)}, f32[]{:T(128)}) all-reduce(f32[]{:T(128)} %get-tuple-element.7, f32[]{:T(128)} %get-tuple-element.6), channel_id=1, replica_groups=mesh['wide'=32,'narrow'=8] {'wide','narrow'}, use_global_device_ids=true, to_apply=%region_1.0 | all-reduce | flops 2 | bytes 16 | tf_op jit(solution)/shard_map/psum | solution.py:80
  125.3 73.5 %psum.44 = f32[]{:T(128)} all-reduce(f32[]{:T(128)} %get-tuple-element.12), channel_id=1, replica_groups=mesh['wide'=32,'narrow'=8] {'wide','narrow'}, use_global_device_ids=true, to_apply=%region_5.0 | all-reduce | flops 1 | bytes 8 | tf_op jit(solution)/shard_map/psum | solution.py:80
  200.4 1.3 collective-permute-start.8
  201.7 4.0 collective-permute-start.9
  206.5 3.7 collective-permute-start.10
  210.3 2.5 collective-permute-start.11
  214.7 77.4 %psum.45 = f32[]{:T(128)} all-reduce(f32[]{:T(128)} %get-tuple-element.10), channel_id=1, replica_groups=mesh['wide'=32,'narrow'=8] {'wide','narrow'}, use_global_device_ids=true, to_apply=%region_7.0 | all-reduce | flops 1 | bytes 8 | tf_op jit(solution)/shard_map/psum | solution.py:108
  295.4 76.6 %psum.46 = f32[]{:T(128)} all-reduce(f32[]{:T(128)} %multiply_reduce_fusion), channel_id=1, replica_groups=mesh['wide'=32,'narrow'=8] {'wide','narrow'}, use_global_device_ids=true, to_apply=%region_9.0 | all-reduce | flops 1 | bytes 8 | tf_op jit(solution)/shard_map/psum | solution.py:80
  373.6 1.6 collective-permute-start.12
  375.2 4.3 collective-permute-start.13
  380.4 3.8 collective-permute-start.14
  384.2 2.1 collective-permute-start.15
  388.3 3.2 slice.488
  391.5 77.5 %psum.47 = f32[]{:T(128)} all-reduce(f32[]{:T(128)} %fusion.38), channel_id=1, replica_groups=mesh['wide'=32,'narrow'=8] {'wide','narrow'}, use_global_device_ids=true, to_apply=%region_11.0 | all-reduce | flops 1 | bytes 8 | tf_op jit(solution)/shard_map/psum | solution.py:108
  470.6 1.3 collective-permute-start.16
  471.9 4.3 collective-permute-start.17
  477.2 3.4 collective-permute-start.18
  480.6 2.1 collective-permute-start.19
  484.0 1.5 maximum_subtract_fusion
  487.6 1.7 constant_dynamic-update-slice_fusion.2
  489.3 6.9 %multiply_add_fusion.1 = (f32[16,16,8,512]{3,0,2,1:T(8,128)S(1)}, f32[16,18,8,512]{3,0,2,1:T(8,128)}) fusion(f32[16,16,8,511]{3,0,2,1:T(8,128)S(1)} %copy-done.4, f32[16,8,512]{2,1,0:T(8,128)S(1)} %get-tuple-element.38, f32[16,8,512]{2,1,0:T(8,128)S(1)} %get-tuple-element.37, f32[16,16,8,512]{3,2,1,0:T(8,128)S(1)} %copy-done.3, ...), kind=kLoop, calls=%fused_computation.33 | loop fusion | flops 3145728 | bytes 17293312 | tf_op jit(solution)/shard_map/add | solution.py:55
  496.2 1.7 constant_dynamic-update-slice_fusion
  497.9 1.4 fusion.56
  499.3 4.2 collective-permute-start.22
  503.5 2.1 collective-permute-start.23
  507.0 3.1 fusion.6
  510.3 4.4 collective-permute-done.23
  514.8 2.3 fusion.4
  517.0 7.3 %fusion.15 = f32[16,16,8,512]{3,0,2,1:T(8,128)S(1)} fusion(f32[16,16,9,512]{3,0,2,1:T(8,128)S(1)} %fusion.4, f32[16,17,8,512]{3,0,2,1:T(8,128)S(1)} %fusion.6, f32[16,16,8,512]{3,0,2,1:T(8,128)S(1)} %get-tuple-element.25, f32[16,16,8,511]{3,0,2,1:T(8,128)S(1)} %bitcast.88, f32[16,16,8,512]{3,2,1,0:T(8,128)S(1)} %copy-done.3), kind=kLoop, calls=%fused_computation.30 | loop fusion | flops 7340032 | bytes 33546240 | tf_op jit(solution)/shard_map/sub | solution.py:58
  524.4 3.7 collective-permute-start.24
  531.5 4.1 collective-permute-done.25
  535.7 5.4 collective-permute-start.26
  541.1 2.3 collective-permute-start.27
  543.4 1.7 multiply_add_fusion
  545.2 1.9 fusion.7
  547.9 4.5 collective-permute-done.27
  552.4 2.0 fusion.1
  554.5 4.0 fusion.11
  558.5 4.4 copy.14
  (126 shorter events, 28.2 us)
Async XLA Ops:
  1.6 27.2 %collective-permute-start.3 = (f32[16,1,512]{2,1,0:T(1,128)S(1)}, f32[16,1,512]{2,1,0:T(1,128)S(1)}, u32[]{:S(2)}, u32[]{:S(2)}) collective-permute-start(f32[16,1,512]{2,1,0:T(1,128)S(1)} %slice_bitcast_fusion.12), channel_id=1, source_target_pairs={{0,1},{1,2},{2,3},{3,4},{4,5},{5,6},{6,7},{8,9},{9,10},{10,11},{11... | collective-permute-start | bytes 98312 | tf_op jit(solution)/shard_map/ppermute | solution.py:29
  6.9 21.9 %collective-permute-start.2 = (f32[1,8,512]{2,1,0:T(8,128)S(1)}, f32[1,8,512]{2,1,0:T(8,128)S(1)}, u32[]{:S(2)}, u32[]{:S(2)}) collective-permute-start(f32[1,8,512]{2,1,0:T(8,128)S(1)} %slice_bitcast_fusion.14), channel_id=1, source_target_pairs={{0,8},{8,16},{16,24},{24,32},{32,40},{40,48},{48,56},{56,64},{64,7... | collective-permute-start | bytes 49160 | tf_op jit(solution)/shard_map/ppermute | solution.py:29
  11.4 17.4 %collective-permute-start.1 = (f32[16,1,512]{2,1,0:T(1,128)S(1)}, f32[16,1,512]{2,1,0:T(1,128)S(1)}, u32[]{:S(2)}, u32[]{:S(2)}) collective-permute-start(f32[16,1,512]{2,1,0:T(1,128)S(1)} %slice_bitcast_fusion.13), channel_id=1, source_target_pairs={{0,1},{1,2},{2,3},{3,4},{4,5},{5,6},{6,7},{8,9},{9,10},{10,11},{11... | collective-permute-start | bytes 98312 | tf_op jit(solution)/shard_map/ppermute | solution.py:29
  14.3 14.3 %copy-start.5 = (f32[3,16,8,512]{3,2,1,0:T(8,128)S(1)}, f32[3,16,8,512]{3,2,1,0:T(8,128)}, u32[]{:S(2)}) copy-start(f32[3,16,8,512]{3,2,1,0:T(8,128)} %param.3) | copy-start | bytes 2359300
  14.3 14.3 %copy-start.7 = (f32[3,16,8,512]{3,2,1,0:T(8,128)S(1)}, f32[3,16,8,512]{3,2,1,0:T(8,128)}, u32[]{:S(2)}) copy-start(f32[3,16,8,512]{3,2,1,0:T(8,128)} %param.4) | copy-start | bytes 2359300
  14.3 14.5 %collective-permute-start = (f32[1,8,512]{2,1,0:T(8,128)S(1)}, f32[1,8,512]{2,1,0:T(8,128)S(1)}, u32[]{:S(2)}, u32[]{:S(2)}) collective-permute-start(f32[1,8,512]{2,1,0:T(8,128)S(1)} %slice_bitcast_fusion.15), channel_id=1, source_target_pairs={{0,8},{8,16},{16,24},{24,32},{32,40},{40,48},{48,56},{56,64},{64,7... | collective-permute-start | bytes 49160 | tf_op jit(solution)/shard_map/ppermute | solution.py:29
  23.4 5.9 %copy-start = (f32[16,16,8,512]{3,0,2,1:T(8,128)}, f32[16,16,8,512]{3,0,2,1:T(8,128)S(1)}, u32[]{:S(2)}) copy-start(f32[16,16,8,512]{3,0,2,1:T(8,128)S(1)} %copy.13) | copy-start | bytes 12582916
  24.3 463.3 %collective-permute-start.20 = (f32[16,1,8,512]{3,0,2,1:T(8,128)}, f32[16,1,8,512]{3,0,2,1:T(8,128)}, u32[]{:S(2)}, u32[]{:S(2)}) collective-permute-start(f32[16,1,8,512]{3,0,2,1:T(8,128)} %get-tuple-element.28), channel_id=1, source_target_pairs={{0,8},{8,16},{16,24},{24,32},{32,40},{40,48},{48,56},{56,64},{64,7... | collective-permute-start | bytes 786440 | tf_op jit(solution)/shard_map/ppermute | solution.py:18
  29.4 6.0 %collective-permute-start.4 = (f32[1,8,512]{2,1,0:T(8,128)S(1)}, f32[1,8,512]{2,1,0:T(8,128)S(1)}, u32[]{:S(2)}, u32[]{:S(2)}) collective-permute-start(f32[1,8,512]{2,1,0:T(8,128)S(1)} %get-tuple-element.58), channel_id=1, source_target_pairs={{8,0},{16,8},{24,16},{32,24},{40,32},{48,40},{56,48},{64,56},{72,6... | collective-permute-start | bytes 49160 | tf_op jit(solution)/shard_map/ppermute | solution.py:21
  30.7 5.5 collective-permute-start.5
  36.3 6.6 %collective-permute-start.6 = (f32[18,1,512]{2,1,0:T(1,128)S(1)}, f32[18,1,512]{2,1,0:T(1,128)S(1)}, u32[]{:S(2)}, u32[]{:S(2)}) collective-permute-start(f32[18,1,512]{2,1,0:T(1,128)S(1)} %get-tuple-element.49), channel_id=1, source_target_pairs={{1,0},{2,1},{3,2},{4,3},{5,4},{6,5},{7,6},{9,8},{10,9},{11,10},{12... | collective-permute-start | bytes 110600 | tf_op jit(solution)/shard_map/ppermute | solution.py:21
  39.8 4.1 collective-permute-start.7
  200.4 5.4 collective-permute-start.8
  201.7 4.8 collective-permute-start.9
  206.5 6.3 %collective-permute-start.10 = (f32[18,1,512]{2,1,0:T(1,128)S(1)}, f32[18,1,512]{2,1,0:T(1,128)S(1)}, u32[]{:S(2)}, u32[]{:S(2)}) collective-permute-start(f32[18,1,512]{2,1,0:T(1,128)S(1)} %get-tuple-element.47), channel_id=1, source_target_pairs={{1,0},{2,1},{3,2},{4,3},{5,4},{6,5},{7,6},{9,8},{10,9},{11,10},{12... | collective-permute-start | bytes 110600 | tf_op jit(solution)/shard_map/ppermute | solution.py:21
  210.3 3.6 collective-permute-start.11
  294.2 202.1 %collective-permute-start.21 = (f32[16,1,8,512]{3,0,2,1:T(8,128)}, f32[16,1,8,512]{3,0,2,1:T(8,128)}, u32[]{:S(2)}, u32[]{:S(2)}) collective-permute-start(f32[16,1,8,512]{3,0,2,1:T(8,128)} %get-tuple-element.27), channel_id=1, source_target_pairs={{8,0},{16,8},{24,16},{32,24},{40,32},{48,40},{56,48},{64,56},{72,6... | collective-permute-start | bytes 786440 | tf_op jit(solution)/shard_map/ppermute | solution.py:21
  373.3 14.9 %copy-start.1 = (f32[16,16,8,512]{3,0,2,1:T(8,128)S(1)}, f32[16,16,8,512]{3,0,2,1:T(8,128)}, u32[]{:S(2)}) copy-start(f32[16,16,8,512]{3,0,2,1:T(8,128)} %copy-done) | copy-start | bytes 12582916
  373.6 6.0 %collective-permute-start.12 = (f32[1,8,512]{2,1,0:T(8,128)S(1)}, f32[1,8,512]{2,1,0:T(8,128)S(1)}, u32[]{:S(2)}, u32[]{:S(2)}) collective-permute-start(f32[1,8,512]{2,1,0:T(8,128)S(1)} %get-tuple-element.54), channel_id=1, source_target_pairs={{8,0},{16,8},{24,16},{32,24},{40,32},{48,40},{56,48},{64,56},{72,6... | collective-permute-start | bytes 49160 | tf_op jit(solution)/shard_map/ppermute | solution.py:21
  375.2 5.2 collective-permute-start.13
  380.4 6.0 %collective-permute-start.14 = (f32[18,1,512]{2,1,0:T(1,128)S(1)}, f32[18,1,512]{2,1,0:T(1,128)S(1)}, u32[]{:S(2)}, u32[]{:S(2)}) collective-permute-start(f32[18,1,512]{2,1,0:T(1,128)S(1)} %get-tuple-element.45), channel_id=1, source_target_pairs={{1,0},{2,1},{3,2},{4,3},{5,4},{6,5},{7,6},{9,8},{10,9},{11,10},{12... | collective-permute-start | bytes 110600 | tf_op jit(solution)/shard_map/ppermute | solution.py:21
  384.2 3.1 collective-permute-start.15
  470.4 15.2 %copy-start.6 = (f32[16,8,512]{2,1,0:T(8,128)}, f32[16,8,512]{2,1,0:T(8,128)S(1)}, u32[]{:S(2)}) copy-start(f32[16,8,512]{2,1,0:T(8,128)S(1)} %multiply_add_fusion.2) | copy-start | bytes 786436
  470.6 5.7 %collective-permute-start.16 = (f32[1,8,512]{2,1,0:T(8,128)S(1)}, f32[1,8,512]{2,1,0:T(8,128)S(1)}, u32[]{:S(2)}, u32[]{:S(2)}) collective-permute-start(f32[1,8,512]{2,1,0:T(8,128)S(1)} %get-tuple-element.52), channel_id=1, source_target_pairs={{8,0},{16,8},{24,16},{32,24},{40,32},{48,40},{56,48},{64,56},{72,6... | collective-permute-start | bytes 49160 | tf_op jit(solution)/shard_map/ppermute | solution.py:21
  471.9 5.2 collective-permute-start.17
  477.1 9.5 %copy-start.18 = (f32[16,1,512]{2,1,0:T(1,128)S(1)}, f32[16,1,512]{2,1,0:T(1,128)}, u32[]{:S(2)}) copy-start(f32[16,1,512]{2,1,0:T(1,128)} %copy-done.17) | copy-start | bytes 98308
  477.2 5.6 collective-permute-start.18
  480.6 3.2 collective-permute-start.19
  484.0 5.3 copy-start.3
  484.0 5.3 copy-start.4
  485.5 3.8 copy-start.10
  485.7 10.5 %copy-start.15 = (f32[16,8,512]{2,1,0:T(8,128)}, f32[16,8,512]{2,1,0:T(8,128)S(1)}, u32[]{:S(2)}) copy-start(f32[16,8,512]{2,1,0:T(8,128)S(1)} %get-tuple-element.38) | copy-start | bytes 786436
  489.3 17.7 %copy-start.2 = (f32[16,16,8,512]{3,0,2,1:T(8,128)S(1)}, f32[16,16,8,512]{3,0,2,1:T(8,128)}, u32[]{:S(2)}) copy-start(f32[16,16,8,512]{3,0,2,1:T(8,128)} %copy-done) | copy-start | bytes 12582916
  499.3 11.0 %collective-permute-start.22 = (f32[16,18,1,512]{3,0,2,1:T(8,128)S(1)}, f32[16,18,1,512]{3,0,2,1:T(8,128)S(1)}, u32[]{:S(2)}, u32[]{:S(2)}) collective-permute-start(f32[16,18,1,512]{3,0,2,1:T(8,128)S(1)} %get-tuple-element.21), channel_id=1, source_target_pairs={{0,1},{1,2},{2,3},{3,4},{4,5},{5,6},{6,7},{8,9},{9,10},{10,11},{11... | collective-permute-start | bytes 1769480 | tf_op jit(solution)/shard_map/ppermute | solution.py:18
  503.5 11.2 %collective-permute-start.23 = (f32[16,18,1,512]{3,0,2,1:T(8,128)S(1)}, f32[16,18,1,512]{3,0,2,1:T(8,128)S(1)}, u32[]{:S(2)}, u32[]{:S(2)}) collective-permute-start(f32[16,18,1,512]{3,0,2,1:T(8,128)S(1)} %get-tuple-element.22), channel_id=1, source_target_pairs={{1,0},{2,1},{3,2},{4,3},{5,4},{6,5},{7,6},{9,8},{10,9},{11,10},{12... | collective-permute-start | bytes 1769480 | tf_op jit(solution)/shard_map/ppermute | solution.py:21
  505.7 9.1 %slice-start = ((s8[4718592]{0:T(1024)(128)(4,1)}), s8[4194304]{0:T(1024)(128)(4,1)S(1)}, s32[]{:S(2)}) async-start(s8[4718592]{0:T(1024)(128)(4,1)} %bitcast.90), calls=%async_computation | async-start | bytes 8388608
  507.0 3.2 copy-start.11
  507.0 3.2 copy-start.13
  507.0 7.7 %slice-start.1 = ((s8[4718592]{0:T(1024)(128)(4,1)}), s8[524288]{0:T(1024)(128)(4,1)S(1)}, s32[]{:S(2)}) async-start(s8[4718592]{0:T(1024)(128)(4,1)} %bitcast.90), calls=%async_computation.1 | async-start | bytes 1048576
  507.0 7.7 %copy-start.8 = (f32[16,9,512]{2,1,0:T(8,128)S(1)}, f32[16,9,512]{2,1,0:T(8,128)}, u32[]{:S(2)}) copy-start(f32[16,9,512]{2,1,0:T(8,128)} %get-tuple-element.42) | copy-start | bytes 884740
  524.4 7.0 %collective-permute-start.24 = (f32[16,1,8,512]{3,0,2,1:T(8,128)S(1)}, f32[16,1,8,512]{3,0,2,1:T(8,128)S(1)}, u32[]{:S(2)}, u32[]{:S(2)}) collective-permute-start(f32[16,1,8,512]{3,0,2,1:T(8,128)S(1)} %get-tuple-element.23), channel_id=1, source_target_pairs={{0,8},{8,16},{16,24},{24,32},{32,40},{40,48},{48,56},{56,64},{64,7... | collective-permute-start | bytes 786440 | tf_op jit(solution)/shard_map/ppermute | solution.py:18
  528.2 7.4 %collective-permute-start.25 = (f32[16,1,8,512]{3,0,2,1:T(8,128)S(1)}, f32[16,1,8,512]{3,0,2,1:T(8,128)S(1)}, u32[]{:S(2)}, u32[]{:S(2)}) collective-permute-start(f32[16,1,8,512]{3,0,2,1:T(8,128)S(1)} %get-tuple-element.24), channel_id=1, source_target_pairs={{8,0},{16,8},{24,16},{32,24},{40,32},{48,40},{56,48},{64,56},{72,6... | collective-permute-start | bytes 786440 | tf_op jit(solution)/shard_map/ppermute | solution.py:21
  530.6 12.8 %copy-start.16 = (f32[16,8,512]{2,1,0:T(8,128)S(1)}, f32[16,8,512]{2,1,0:T(8,128)}, u32[]{:S(2)}) copy-start(f32[16,8,512]{2,1,0:T(8,128)} %copy-done.15) | copy-start | bytes 786436
  535.7 12.2 %collective-permute-start.26 = (f32[16,18,1,512]{3,0,2,1:T(8,128)S(1)}, f32[16,18,1,512]{3,0,2,1:T(8,128)S(1)}, u32[]{:S(2)}, u32[]{:S(2)}) collective-permute-start(f32[16,18,1,512]{3,0,2,1:T(8,128)S(1)} %get-tuple-element.19), channel_id=1, source_target_pairs={{0,1},{1,2},{2,3},{3,4},{4,5},{5,6},{6,7},{8,9},{9,10},{10,11},{11... | collective-permute-start | bytes 1769480 | tf_op jit(solution)/shard_map/ppermute | solution.py:18
  541.1 4.0 copy-start.12
  541.1 4.0 copy-start.14
  541.1 11.3 %collective-permute-start.27 = (f32[16,18,1,512]{3,0,2,1:T(8,128)S(1)}, f32[16,18,1,512]{3,0,2,1:T(8,128)S(1)}, u32[]{:S(2)}, u32[]{:S(2)}) collective-permute-start(f32[16,18,1,512]{3,0,2,1:T(8,128)S(1)} %get-tuple-element.20), channel_id=1, source_target_pairs={{1,0},{2,1},{3,2},{4,3},{5,4},{6,5},{7,6},{9,8},{10,9},{11,10},{12... | collective-permute-start | bytes 1769480 | tf_op jit(solution)/shard_map/ppermute | solution.py:21
  545.1 7.3 %copy-start.9 = (f32[16,9,512]{2,1,0:T(8,128)S(1)}, f32[16,9,512]{2,1,0:T(8,128)}, u32[]{:S(2)}) copy-start(f32[16,9,512]{2,1,0:T(8,128)} %get-tuple-element.42) | copy-start | bytes 884740
  (1 other events, 0.6 us)
where the time goes:
time: 568 us; the launch traced here: 563 us
  blocking collectives  383 us (67%)
  starting transfers between devices  85.5 us (15%)
  other arithmetic  39.6 us (7%)
  local copies, waits for them, and re-layouts  24.2 us (4%)
  waiting for transfers between devices  22 us (4%)
  between operations  8.22 us (1%)
    psum x3, blocking collectives, precond_norm(): return lax.psum(jnp.sum(residual * precond), ('wide', 'narrow'))  228 us
    psum x2, blocking collectives, body(): alpha = inner / lax.psum(jnp.sum(direction * image), ('wide', 'narrow'))  155 us
    ppermute x12, starting transfers between devices, with_halo(): lax.ppermute(lax.slice_in_dim(block, block.shape[dim] - width, None, axis...  44.6 us
    ppermute x12, starting transfers between devices, with_halo(): lax.ppermute(lax.slice_in_dim(block, 0, width, axis=dim), axis, backward)  26.9 us
    ppermute x4, starting transfers between devices, shifted(): return lax.ppermute(value, axis, pairs)  13.9 us
    ppermute x12, waiting for transfers between devices, with_halo(): lax.ppermute(lax.slice_in_dim(block, 0, width, axis=dim), axis, backward)  13.1 us
    unnamed x45, local copies, waits for them, and re-layouts  11.7 us
  transfers between devices with their start and end apart: 28, of which 14 were waited for; matrix products, arithmetic and copies ran while one was open for 7% of the time, Pallas kernels for 0%

commit v1 on v0

v1 whole, which is shorter than its diff:
```python
import functools

import jax
import jax.numpy as jnp
from jax import lax
from jax.experimental import pallas as pl
from jax.experimental.pallas import tpu as pltpu
from jax.sharding import PartitionSpec as P

MESH = pl.DeviceIdType.MESH
F32 = jnp.float32
COURANT = 0.15

PLANES = 16
CH = 4
PR = CH * 8
OWN = PLANES * PR
EDGE = PLANES * CH
TR = 16
CHUNKS = 4
PER = TR // CHUNKS
NWIDE = 32
NNARROW = 8
SHIFT = 1.0


def lane_id():
    return lax.broadcasted_iota(jnp.int32, (8, 128), 1)


def sub_id():
    return lax.broadcasted_iota(jnp.int32, (8, 128), 0)


def next_k(xs):
    last = lane_id() == 127
    r = [pltpu.roll(x, 127, 1) for x in xs]
    zero = jnp.zeros((8, 128), F32)
    return [jnp.where(last, r[c + 1] if c + 1 < CH else zero, r[c]) for c in range(CH)]


def below_k(xs):
    first = lane_id() == 0
    r = [pltpu.roll(x, 1, 1) for x in xs]
    zero = jnp.zeros((8, 128), F32)
    return [jnp.where(first, r[c - 1] if c else zero, r[c]) for c in range(CH)]


def next_j(xs, edge):
    last = sub_id() == 7
    return [jnp.where(last, edge[c], pltpu.roll(xs[c], 7, 0)) for c in range(CH)]


def below_j(xs, edge):
    first = sub_id() == 0
    return [jnp.where(first, edge[c], pltpu.roll(xs[c], 1, 0)) for c in range(CH)]


def packed_next_k(x):
    r = pltpu.roll(x, 127, 1)
    up = jnp.where((sub_id() & 3) == 3, 0.0, pltpu.roll(r, 7, 0))
    return jnp.where(lane_id() == 127, up, r)


def packed_below_k(x):
    r = pltpu.roll(x, 1, 1)
    down = jnp.where((sub_id() & 3) == 0, 0.0, pltpu.roll(r, 1, 0))
    return jnp.where(lane_id() == 0, down, r)


def at_plane(i, c):
    if isinstance(i, int):
        return pl.ds(i * PR + c * 8, 8)
    return pl.ds(pl.multiple_of(i * PR + c * 8, 8), 8)


def plane(ref, i):
    return [ref[at_plane(i, c), :] for c in range(CH)]


def put_plane(ref, i, xs):
    for c in range(CH):
        ref[at_plane(i, c), :] = xs[c]


def edge_rows(ref, r):
    return [jnp.broadcast_to(ref[pl.ds(r + c, 1), :], (8, 128)) for c in range(CH)]


def mul(xs, ys):
    return [x * y for x, y in zip(xs, ys)]


def add(xs, ys):
    return [x + y for x, y in zip(xs, ys)]


def sub(xs, ys):
    return [x - y for x, y in zip(xs, ys)]


def total(xs):
    return (xs[0] + xs[1]) + (xs[2] + xs[3])


def weights(vx, vxd, vy, vyd, vz, vzd):
    pos = lambda v: [jnp.maximum(x, 0.0) * COURANT for x in v]
    neg = lambda v: [jnp.minimum(x, 0.0) * -COURANT for x in v]
    out = []
    keep = None
    for v, vd in ((vx, vxd), (vy, vyd), (vz, vzd)):
        up, down = neg(v), pos(vd)
        leave = add(pos(v), neg(vd))
        keep = leave if keep is None else add(keep, leave)
        out += [up, down]
    return [[1.0 - x for x in keep]] + out


def apply_weights(k, c, xu, xd, yu, yd, zu, zd):
    out = []
    for q in range(len(c)):
        s = k[0][q] * c[q] + k[1][q] * xu[q]
        s2 = k[2][q] * xd[q] + k[3][q] * yu[q]
        s3 = k[4][q] * yd[q] + k[5][q] * zu[q]
        out.append((s + s2) + (s3 + k[6][q] * zd[q]))
    return out


def transport_plane(k, field, i, low_ref, high_ref, r):
    c = plane(field, i)
    xu, xd = plane(field, i + 1), plane(field, i - 1)
    yu, yd = next_j(c, edge_rows(high_ref, r)), below_j(c, edge_rows(low_ref, r))
    return apply_weights(k, c, xu, xd, yu, yd, next_k(c), below_k(c))


def pressure_kernel(
    co_h, pv_h, tr_h,
    p_o, vel_o, k_o, c1_o, c1n_o,
    cxe, cy, cz, pxe, py, pz, low_n, e1_send,
    rhs_s, inv_s, a0_s, v_s, vn_send, vn_recv,
    red_send, red_recv,
    pe, pn, vx, vy, vz, vyl, pn0, e5_send, e5_recv, kn, kedge,
    te, t_send, t_r1, t_r2,
    lsem, ssem, rsem, red_ss, red_rs,
):
    w, n = lax.axis_index("wide"), lax.axis_index("narrow")
    has = {
        (1, 0): w < NWIDE - 1, (-1, 0): w > 0, (0, 1): n < NNARROW - 1, (0, -1): n > 0,
    }
    for a in (1, -1):
        for b in (1, -1):
            has[(a, b)] = jnp.logical_and(has[(a, 0)], has[(0, b)])

    loads = [
        pltpu.make_async_copy(src, dst, lsem.at[q])
        for q, (src, dst) in enumerate((
            (co_h.at[1], cy), (pv_h.at[1], py),
            (co_h.at[0], cxe.at[pl.ds(PR, OWN)]), (pv_h.at[0], pxe.at[pl.ds(PR, OWN)]),
            (co_h.at[2], cz), (pv_h.at[2], pz),
            (tr_h, te.at[:, pl.ds(2 * PR, OWN)]),
        ))
    ]
    for copy in loads:
        copy.start()

    y, z = lax.div(w, 8), lax.rem(w, 8)
    group_n = [(w, lax.rem(n + e, 8)) for e in (4, 5, 3, 6, 2, 7, 1)]
    offsets = [(a, b) for a in range(4) for b in range(8) if (a, b) != (0, 0)]
    offsets.sort(key=lambda o: -(min(o[0], 4 - o[0]) + min(o[1], 8 - o[1])))
    group_w = [(lax.rem(y + a, 4) * 8 + lax.rem(z + b, 8), n) for a, b in offsets]
    diagonal = [
        (lax.rem(w + a + NWIDE, NWIDE), lax.rem(n + b + NNARROW, NNARROW)) for a in (1, -1) for b in (1, -1)
    ]
    peers = group_w + group_n + diagonal
    barrier = pltpu.get_barrier_semaphore()
    for a, b in peers:
        pl.semaphore_signal(barrier, inc=1, device_id={"wide": a, "narrow": b}, device_id_type=MESH)

    sent = []
    index = [0]

    def message(src, dst, way):
        q = index[0]
        index[0] += 1
        copy = pltpu.make_async_remote_copy(
            src_ref=src, dst_ref=dst, send_sem=ssem.at[q], recv_sem=rsem.at[q],
            device_id={"wide": w + way[0], "narrow": n + way[1]}, device_id_type=MESH,
        )
        back = (-way[0], -way[1])

        @pl.when(has[way])
        def _():
            copy.start()

        sent.append((copy, way))

        def arrive():
            @pl.when(has[back])
            def _():
                copy.wait_recv()

        return arrive

    def blank(dst, way):
        @pl.when(jnp.logical_not(has[way]))
        def _():
            dst[...] = jnp.zeros(dst.shape, F32)

    for ref, dst in ((cxe, pl.ds(0, PR)), (pxe, pl.ds(0, PR))):
        blank(ref.at[dst], (-1, 0))
    blank(low_n.at[0], (0, -1))
    blank(low_n.at[1], (0, -1))
    for s in range(3):
        blank(v_s.at[s, pl.ds(0, PR)], (-1, 0))
        blank(v_s.at[s, pl.ds(17 * PR, PR)], (1, 0))
        blank(vn_recv.at[s, 0], (0, -1))
        blank(vn_recv.at[s, 1], (0, 1))
    for ref, low, high in ((vx, 0, 18), (vy, 0, 17), (vz, 0, 17)):
        blank(ref.at[pl.ds(low * PR, PR)], (-1, 0))
        blank(ref.at[pl.ds(high * PR, PR)], (1, 0))
    blank(vyl.at[pl.ds(0, 8)], (-1, 0))
    blank(vyl.at[pl.ds(8 + EDGE, 8)], (1, 0))
    blank(e5_recv.at[0], (0, -1))
    blank(e5_recv.at[1], (0, 1))

    def blank_tracers(t, _):
        blank(te.at[t, pl.ds(0, 2 * PR)], (-1, 0))
        blank(te.at[t, pl.ds(18 * PR, 2 * PR)], (1, 0))
        for side, b in ((0, -1), (1, 1)):
            blank(t_r1.at[side, t, pl.ds(8, EDGE)], (0, b))
            blank(t_r2.at[side, t], (0, b))
            blank(t_r1.at[side, t, pl.ds(0, 8)], (-1, b))
            blank(t_r1.at[side, t, pl.ds(8 + EDGE, 8)], (1, b))
        return 0

    lax.fori_loop(0, TR, blank_tracers, 0)

    pl.semaphore_wait(barrier, len(peers))

    def pack(src, base, j):
        return src[pl.ds(base + j, EDGE, stride=8), :]

    got = [
        message(co_h.at[0, pl.ds(OWN - PR, PR)], cxe.at[pl.ds(0, PR)], (1, 0)),
        message(pv_h.at[0, pl.ds(OWN - PR, PR)], pxe.at[pl.ds(0, PR)], (1, 0)),
    ]
    loads[0].wait()
    e1_send[0] = pack(cy, 0, 7)
    loads[1].wait()
    e1_send[1] = pack(py, 0, 7)
    got.append(message(e1_send, low_n, (0, 1)))

    bulk = []

    def send_bulk(chunk):
        t0 = chunk * PER

        def rows(t, _):
            for slot, j in enumerate((0, 1, 6, 7)):
                t_send[slot, t] = te[t, pl.ds(2 * PR + j, EDGE, stride=8), :]
            return 0

        lax.fori_loop(t0, t0 + PER, rows, 0)
        ts = pl.ds(t0, PER)
        main = pl.ds(8, EDGE)
        bulk.extend([
            message(t_send.at[3, ts], t_r1.at[0, ts, main], (0, 1)),
            message(t_send.at[0, ts], t_r1.at[1, ts, main], (0, -1)),
            message(te.at[ts, pl.ds(16 * PR, 2 * PR)], te.at[ts, pl.ds(0, 2 * PR)], (1, 0)),
            message(te.at[ts, pl.ds(2 * PR, 2 * PR)], te.at[ts, pl.ds(18 * PR, 2 * PR)], (-1, 0)),
            message(t_send.at[2, ts], t_r2.at[0, ts], (0, 1)),
            message(t_send.at[1, ts], t_r2.at[1, ts], (0, -1)),
        ])

    def send_corners():
        low, high = pl.ds(0, 8), pl.ds(8 + EDGE, 8)
        first, last = pl.ds(0, 8), pl.ds(EDGE - 8, 8)
        bulk.extend([
            message(t_send.at[3, :, last], t_r1.at[0, :, low], (1, 1)),
            message(t_send.at[3, :, first], t_r1.at[0, :, high], (-1, 1)),
            message(t_send.at[0, :, last], t_r1.at[1, :, low], (1, -1)),
            message(t_send.at[0, :, first], t_r1.at[1, :, high], (-1, -1)),
        ])

    loads[6].wait()
    send_bulk(0)
    for copy in loads[2:6]:
        copy.wait()
    for arrive in got:
        arrive()

    zero = jnp.zeros((8, 128), F32)

    def start_plane(i, acc):
        cxu, cxd = plane(cxe, i + 1), plane(cxe, i)
        cyu, czu = plane(cy, i), plane(cz, i)
        cyd = below_j(cyu, edge_rows(low_n.at[0], i * CH))
        czd = below_k(czu)
        diag = add(add(add(cxu, cxd), add(cyu, cyd)), add(czu, czd))
        pyu, pzu = plane(py, i), plane(pz, i)
        pyd = below_j(pyu, edge_rows(low_n.at[1], i * CH))
        d = sub(plane(pxe, i + 1), plane(pxe, i))
        d = add(add(d, sub(pyu, pyd)), sub(pzu, below_k(pzu)))
        rhs = [-x for x in d]
        inv = [1.0 / x for x in diag]
        v = mul(rhs, inv)
        put_plane(rhs_s, i, rhs)
        put_plane(inv_s, i, inv)
        put_plane(v_s.at[0], i + 1, v)
        return acc + total(mul(rhs, v))

    b0 = lax.fori_loop(0, PLANES, start_plane, zero)

    def exchange(s):
        v = v_s.at[s]
        for slot, j in ((0, 0), (1, 7)):
            vn_send[s, slot] = pack(v, PR, j)
        return [
            message(v.at[pl.ds(PR * 16, PR)], v.at[pl.ds(0, PR)], (1, 0)),
            message(v.at[pl.ds(PR, PR)], v.at[pl.ds(PR * 17, PR)], (-1, 0)),
            message(vn_send.at[s, 1], vn_recv.at[s, 0], (0, 1)),
            message(vn_send.at[s, 0], vn_recv.at[s, 1], (0, -1)),
        ]

    def image(s, i):
        v_ref = v_s.at[s]
        v = plane(v_ref, i + 1)
        vu, vd = plane(v_ref, i + 2), plane(v_ref, i)
        fx = mul(plane(cxe, i + 1), sub(vu, v))
        fxd = mul(plane(cxe, i), sub(v, vd))
        low, high = edge_rows(vn_recv.at[s, 0], i * CH), edge_rows(vn_recv.at[s, 1], i * CH)
        fy = mul(plane(cy, i), sub(next_j(v, high), v))
        edge = mul(edge_rows(low_n.at[0], i * CH), sub(v, low))
        fyd = below_j(fy, edge)
        fz = mul(plane(cz, i), sub(next_k(v), v))
        a = add(add(sub(fxd, fx), sub(fyd, fy)), sub(below_k(fz), fz))
        return v, a

    got = exchange(0)
    send_bulk(1)
    for arrive in got:
        arrive()

    def first_plane(i, acc):
        v, a = image(0, i)
        put_plane(a0_s, i, a)
        new = sub(mul(a, plane(inv_s, i)), [x * SHIFT for x in v])
        put_plane(v_s.at[1], i + 1, new)
        g00, g01, b1 = acc
        return g00 + total(mul(v, a)), g01 + total(mul(new, a)), b1 + total(mul(new, plane(rhs_s, i)))

    g00, g01, b1 = lax.fori_loop(0, PLANES, first_plane, (zero, zero, zero))
    got = exchange(1)
    send_bulk(2)
    for arrive in got:
        arrive()

    def second_plane(i, acc):
        v, a = image(1, i)
        new = sub(mul(a, plane(inv_s, i)), [x * SHIFT for x in v])
        put_plane(v_s.at[2], i + 1, new)
        g11, g12, g02, b2 = acc
        return (
            g11 + total(mul(v, a)), g12 + total(mul(new, a)),
            g02 + total(mul(new, plane(a0_s, i))), b2 + total(mul(new, plane(rhs_s, i))),
        )

    g11, g12, g02, b2 = lax.fori_loop(0, PLANES, second_plane, (zero,) * 4)
    got = exchange(2)
    send_bulk(3)

    lane = lax.broadcasted_iota(jnp.int32, (1, 128), 1)

    def place(x, m):
        s = jnp.sum(jnp.sum(x, axis=0, keepdims=True), axis=1, keepdims=True)
        return jnp.where(lane == m, s, 0.0)

    sums = jnp.zeros((1, 128), F32)
    for m, x in enumerate((b0, b1, b2, g00, g01, g02, g11, g12)):
        sums = sums + place(x, m)
    for arrive in got:
        arrive()

    def third_plane(i, g22):
        v, a = image(2, i)
        return g22 + total(mul(v, a))

    sums = sums + place(lax.fori_loop(0, PLANES, third_plane, zero), 8)

    pending = []
    for g, group in enumerate((group_n, group_w)):
        red_send[g] = sums
        copies = []
        for q, (a, b) in enumerate(group):
            copy = pltpu.make_async_remote_copy(
                src_ref=red_send.at[g], dst_ref=red_recv.at[g, q],
                send_sem=red_ss.at[g, q], recv_sem=red_rs.at[g, q],
                device_id={"wide": a, "narrow": b}, device_id_type=MESH,
            )
            copy.start()
            copies.append(copy)
        if g == 0:
            send_corners()
        for copy in copies:
            copy.wait_recv()
        sums = sums + jnp.sum(red_recv[g, 0 : len(group)], axis=0)
        pending += copies

    b0, b1, b2, g00, g01, g02, g11, g12, g22 = [sums[:, m : m + 1] for m in range(9)]
    ratio = lambda a, b: jnp.where(b > 0.0, a / b, 0.0)
    l1 = g01 / g00
    l2 = g02 / g00
    d1 = g11 - l1 * g01
    t = g12 - l2 * g01
    l3 = ratio(t, d1)
    d2 = g22 - l2 * g02 - l3 * t
    y1 = b1 - l1 * b0
    y2 = b2 - l2 * b0 - l3 * y1
    q2 = ratio(y2, d2)
    q1 = ratio(y1, d1) - l3 * q2
    q0 = b0 / g00 - l1 * q1 - l2 * q2
    q0, q1, q2 = [jnp.broadcast_to(q, (8, 128)) for q in (q0, q1, q2)]

    def combine(i, _):
        vs = [plane(v_s.at[s], i) for s in range(3)]
        put_plane(pe, i, [q0 * vs[0][c] + q1 * vs[1][c] + q2 * vs[2][c] for c in range(CH)])
        return 0

    lax.fori_loop(0, PLANES + 2, combine, 0)
    for side in range(2):
        for r in range(EDGE // 8):
            rows = pl.ds(r * 8, 8)
            pn[side, rows] = (
                q0 * vn_recv[0, side, rows] + q1 * vn_recv[1, side, rows] + q2 * vn_recv[2, side, rows]
            )

    def low_x():
        p0, p1 = plane(pe, 0), plane(pe, 1)
        put_plane(vx, 1, sub(plane(pxe, 0), mul(plane(cxe, 0), sub(p1, p0))))

    low_x()
    vyl[pl.ds(8, EDGE), :] = low_n[1] - low_n[0] * (pack(pe, PR, 0) - pn[0])

    def velocity_plane(i, _):
        p = plane(pe, i + 1)
        put_plane(p_o, i, p)
        ux = sub(plane(pxe, i + 1), mul(plane(cxe, i + 1), sub(plane(pe, i + 2), p)))
        uy = sub(plane(py, i), mul(plane(cy, i), sub(next_j(p, edge_rows(pn.at[1], i * CH)), p)))
        uz = sub(plane(pz, i), mul(plane(cz, i), sub(next_k(p), p)))
        for d, u in enumerate((ux, uy, uz)):
            put_plane(vel_o.at[d], i, u)
        put_plane(vx, i + 2, ux)
        put_plane(vy, i + 1, uy)
        put_plane(vz, i + 1, uz)
        return 0

    lax.fori_loop(0, PLANES, velocity_plane, 0)

    one = lambda i: pl.ds(i * PR, PR)
    got = [
        message(vx.at[one(16)], vx.at[one(0)], (1, 0)),
        message(vx.at[one(2)], vx.at[one(18)], (-1, 0)),
        message(vy.at[one(16)], vy.at[one(0)], (1, 0)),
        message(vy.at[one(1)], vy.at[one(17)], (-1, 0)),
        message(vz.at[one(16)], vz.at[one(0)], (1, 0)),
        message(vz.at[one(1)], vz.at[one(17)], (-1, 0)),
        message(vyl.at[pl.ds(EDGE, 8)], vyl.at[pl.ds(0, 8)], (1, 0)),
        message(vyl.at[pl.ds(8, 8)], vyl.at[pl.ds(8 + EDGE, 8)], (-1, 0)),
    ]
    for slot, j in ((0, 0), (1, 7)):
        e5_send[slot, pl.ds(0, EDGE)] = pack(vy, PR, 0 if slot == 0 else 6)
        e5_send[slot, pl.ds(EDGE, 8)] = zero
        e5_send[slot, pl.ds(EDGE + 4, 4)] = vx[pl.ds(PR + j, CH, stride=8), :]
        e5_send[slot, pl.ds(EDGE + 8, EDGE)] = pack(vx, 2 * PR, j)
        e5_send[slot, pl.ds(2 * EDGE + 8, EDGE)] = pack(vz, PR, j)
    got.append(message(e5_send.at[1], e5_recv.at[0], (0, 1)))
    got.append(message(e5_send.at[0], e5_recv.at[1], (0, -1)))

    for arrive in bulk:
        arrive()

    def plane_weights(i):
        uy, uz = plane(vy, i + 1), plane(vz, i + 1)
        uyd = below_j(uy, edge_rows(vyl, 8 + i * CH))
        return weights(plane(vx, i + 2), plane(vx, i + 1), uy, uyd, uz, below_k(uz))

    def step_plane(i, k):
        for t in range(TR):
            out = transport_plane(k, te.at[t], i + 2, t_r1.at[0, t], t_r1.at[1, t], 8 + i * CH)
            put_plane(c1_o.at[t], i + 1, out)

    def own_plane(i, _):
        k = plane_weights(i)
        for m in range(7):
            put_plane(k_o.at[m], i, k[m])
        step_plane(i, k)
        return 0

    lax.fori_loop(0, PLANES, own_plane, 0)
    for arrive in got:
        arrive()

    for i, way in ((-1, (-1, 0)), (PLANES, (1, 0))):
        inside = jnp.where(has[way], 1.0, 0.0)
        k = [[x * inside for x in m] for m in plane_weights(i)]
        step_plane(i, k)

    kedge[0] = pack(vy, PR, 7)
    for side, way in ((0, (0, -1)), (1, (0, 1))):
        inside = jnp.where(has[way], 1.0, 0.0)
        for r in range(EDGE // 8):
            ev = e5_recv.at[side]
            far = ev[pl.ds(r * 8, 8), :]
            ux, uxd = ev[pl.ds(EDGE + 8 + r * 8, 8), :], ev[pl.ds(EDGE + 4 + r * 8, 8), :]
            uz = ev[pl.ds(2 * EDGE + 8 + r * 8, 8), :]
            if side == 0:
                uy, uyd = vyl[pl.ds(8 + r * 8, 8), :], far
            else:
                uy, uyd = far, kedge[0, pl.ds(r * 8, 8), :]
            k = weights([ux], [uxd], [uy], [uyd], [uz], [packed_below_k(uz)])
            k = [[m[0] * inside] for m in k]

            def row_step(t, _, side=side, r=r, k=k):
                ref = t_r1.at[side, t]
                c = ref[pl.ds(8 + r * 8, 8), :]
                xu, xd = ref[pl.ds(12 + r * 8, 8), :], ref[pl.ds(4 + r * 8, 8), :]
                far = t_r2[side, t, pl.ds(r * 8, 8), :]
                near = t_send[0 if side == 0 else 3, t, pl.ds(r * 8, 8), :]
                yu, yd = (near, far) if side == 0 else (far, near)
                out = apply_weights(k, [c], [xu], [xd], [yu], [yd], [packed_next_k(c)], [packed_below_k(c)])
                c1n_o[side, t, pl.ds(r * 8, 8), :] = out[0]
                return 0

            lax.fori_loop(0, TR, row_step, 0, unroll=8)

    for copy in pending:
        copy.wait_send()
    for copy, way in sent:
        @pl.when(has[way])
        def _(copy=copy):
            copy.wait_send()


def transport_kernel(k_ref, c1, c1n, p, vel, p_h, vel_h, tr_h, out, sem):
    first = [pltpu.make_async_copy(p, p_h, sem.at[0]), pltpu.make_async_copy(vel, vel_h, sem.at[1])]
    for copy in first:
        copy.start()
    copies = []
    parts = 4
    for part in range(parts):

        def own_plane(i, _):
            k = [plane(k_ref.at[m], i) for m in range(7)]
            for t in range(TR):
                put_plane(out.at[t], i, transport_plane(k, c1.at[t], i + 1, c1n.at[0, t], c1n.at[1, t], i * CH))
            return 0

        each = PLANES // parts
        lax.fori_loop(part * each, (part + 1) * each, own_plane, 0)
        rows = pl.ds(part * each * PR, each * PR)
        copy = pltpu.make_async_copy(out.at[:, rows], tr_h.at[:, rows], sem.at[2 + part])
        copy.start()
        copies.append(copy)
    for copy in first + copies:
        copy.wait()


def view(x):
    lead = x.shape[:-3]
    x = x.reshape(x.shape[:-1] + (CH, 128)).swapaxes(-3, -2)
    return x.reshape(lead + (OWN, 128))


def unview(x):
    lead = x.shape[:-2]
    x = x.reshape(lead + (PLANES, CH, 8, 128)).swapaxes(-3, -2)
    return x.reshape(lead + (PLANES, 8, CH * 128))


def body(coefficients, predicted_velocity, tracers):
    shape = lambda *s: jax.ShapeDtypeStruct(s, F32)
    vm = lambda *s: pltpu.VMEM(s, F32)
    hbm = pl.BlockSpec(memory_space=pltpu.HBM)
    vmem = pl.BlockSpec(memory_space=pltpu.VMEM)
    p, vel, k, c1, c1n = pl.pallas_call(
        pressure_kernel,
        out_shape=[
            shape(OWN, 128), shape(3, OWN, 128), shape(7, OWN, 128),
            shape(TR, 18 * PR, 128), shape(2, TR, EDGE, 128),
        ],
        in_specs=[hbm] * 3,
        out_specs=[vmem] * 5,
        scratch_shapes=[
            vm(OWN + PR, 128), vm(OWN, 128), vm(OWN, 128), vm(OWN + PR, 128), vm(OWN, 128), vm(OWN, 128),
            vm(2, EDGE, 128), vm(2, EDGE, 128),
            vm(OWN, 128), vm(OWN, 128), vm(OWN, 128), vm(3, 18 * PR, 128),
            vm(3, 2, EDGE, 128), vm(3, 2, EDGE, 128),
            vm(2, 1, 128), vm(2, 31, 1, 128),
            vm(18 * PR, 128), vm(2, EDGE, 128),
            vm(19 * PR, 128), vm(18 * PR, 128), vm(18 * PR, 128), vm(16 + EDGE, 128), vm(EDGE, 128),
            vm(2, 3 * EDGE + 8, 128), vm(2, 3 * EDGE + 8, 128), vm(7, 8, 128), vm(1, EDGE, 128),
            vm(TR, 20 * PR, 128), vm(4, TR, EDGE, 128), vm(2, TR, 16 + EDGE, 128), vm(2, TR, EDGE, 128),
            pltpu.SemaphoreType.DMA((7,)), pltpu.SemaphoreType.DMA((64,)), pltpu.SemaphoreType.DMA((64,)),
            pltpu.SemaphoreType.DMA((2, 31)), pltpu.SemaphoreType.DMA((2, 31)),
        ],
        compiler_params=pltpu.CompilerParams(
            collective_id=0, has_side_effects=True, vmem_limit_bytes=40 << 20
        ),
    )(view(coefficients), view(predicted_velocity), view(tracers))
    p, vel, tr = pl.pallas_call(
        transport_kernel,
        out_shape=[shape(OWN, 128), shape(3, OWN, 128), shape(TR, OWN, 128)],
        in_specs=[vmem] * 5,
        out_specs=[hbm] * 3,
        scratch_shapes=[vm(TR, OWN, 128), pltpu.SemaphoreType.DMA((6,))],
        compiler_params=pltpu.CompilerParams(vmem_limit_bytes=40 << 20),
    )(k, c1, c1n, p, vel)
    return unview(p), unview(vel), unview(tr)


def solution(mesh):
    placed = (P(None, "wide", "narrow", None),) * 3
    return jax.shard_map(
        body,
        mesh=mesh,
        in_specs=placed,
        out_specs=(P("wide", "narrow", None),) + placed[:2],
        check_vma=False,
    )
```

time: 568 us -> 65.9 us (0.12)
  blocking collectives: 383 us -> 0 us
  starting transfers between devices: 85.5 us -> 0 us
  Pallas kernels: 0 us -> 60.6 us
  other arithmetic: 39.6 us -> 0 us
  waiting for transfers between devices: 22 us -> 0 us
  local copies, waits for them, and re-layouts: 24.2 us -> 4.45 us
  between operations: 8.22 us -> 0.65 us
    psum x5 -> x0, blocking collectives: 383 us -> none  [the longest x3 228 us: precond_norm(): return lax.psum(jnp.sum(residual * precond), ('wide', 'narrow'))]
    ppermute x28 -> x0, starting transfers between devices: 85.5 us -> none  [the longest x12 44.6 us: with_halo(): lax.ppermute(lax.slice_in_dim(block, block.shape[dim] - width, None, axis...]
    pallas_call x0 -> x2, Pallas kernels: none -> 60.6 us  [the longest x1 55.9 us: body(): pl.pallas_call(pressure_kernel, out_shape=[shape(OWN, 128), shape(3, OWN,...]
    ppermute x28 -> x0, waiting for transfers between devices: 22 us -> none  [the longest x12 13.1 us: with_halo(): lax.ppermute(lax.slice_in_dim(block, 0, width, axis=dim), axis, backward)]
    add x9 -> x0, other arithmetic: 18.1 us -> none  [the longest x2 8.61 us: upwind_step(): flux = jnp.maximum(speed, 0.0) * inner + jnp.minimum(speed, 0.0) * above]
    sub x5 -> x0, other arithmetic: 12.8 us -> none  [the longest x2 11.3 us: upwind_step(): return inner - COURANT * change]
    unnamed x45 -> x6, local copies, waits for them, and re-layouts: 11.7 us -> 4.45 us
    slice x14 -> x0, local copies, waits for them, and re-layouts: 7.19 us -> none  [the longest x2 4.32 us: upwind_step(): inner[..., 1:]]
  transfers between devices with their start and end apart: 28 -> 0, of which waited for: 14 -> 0; matrix products, arithmetic and copies ran while one was open for 7% -> 0% of each run, Pallas kernels for 0% -> 0%
where the time goes in v1:
time: 65.9 us; the launch traced here: 65.7 us
  Pallas kernels  60.6 us (92%)
  local copies, waits for them, and re-layouts  4.45 us (7%)
    pallas_call x1, Pallas kernels, body(): pl.pallas_call(pressure_kernel, out_shape=[shape(OWN, 128), shape(3, OWN,...  55.9 us
    pallas_call x1, Pallas kernels, body(): pl.pallas_call(transport_kernel, out_shape=[shape(OWN, 128), shape(3, OWN...  4.68 us
    unnamed x6, local copies, waits for them, and re-layouts  4.45 us

profile of v1, /device:TPU:1, one launch (start us, length us, event | category | flops | bytes accessed | tf_op | source)
XLA Modules:
  0.0 65.7 jit_solution(3671056909001231869)
XLA Ops:
  0.6 0.0 copy-start
  0.6 2.2 %copy-done = f32[16,16,8,512]{3,2,1,0:T(8,128)S(1)} copy-done((f32[16,16,8,512]{3,2,1,0:T(8,128)S(1)}, f32[16,16,8,512]{3,2,1,0:T(8,128)}, u32[]{:S(2)}) %copy-start) | copy-done | bytes 4194328
  2.8 0.0 copy-start.1
  2.8 1.1 %copy-done.1 = f32[3,16,8,512]{3,2,1,0:T(8,128)S(1)} copy-done((f32[3,16,8,512]{3,2,1,0:T(8,128)S(1)}, f32[3,16,8,512]{3,2,1,0:T(8,128)}, u32[]{:S(2)}) %copy-start.1) | copy-done | bytes 786456
  4.0 0.0 copy-start.2
  4.0 1.1 %copy-done.2 = f32[3,16,8,512]{3,2,1,0:T(8,128)S(1)} copy-done((f32[3,16,8,512]{3,2,1,0:T(8,128)S(1)}, f32[3,16,8,512]{3,2,1,0:T(8,128)}, u32[]{:S(2)}) %copy-start.2) | copy-done | bytes 786456
  5.1 55.9 %shard_map.58 = (f32[512,128]{1,0:T(8,128)S(1)}, f32[3,512,128]{2,1,0:T(8,128)S(1)}, f32[7,512,128]{2,1,0:T(8,128)S(1)}, f32[16,576,128]{2,1,0:T(8,128)S(1)}, f32[2,16,64,128]{3,2,1,0:T(8,128)S(1)}) custom-call(f32[3,512,128]{2,1,0:T(8,128)S(1)} %bitcast.31, f32[3,512,128]{2,1,0:T(8,128)S(1)} %bitcast.32, f32[16,512,128]{2,1,0:T(8,128)S(1)} %bitcast.30), custom_call_target="tpu_custom_call" | custom-call | tf_op jit(solution)/shard_map/pallas_call | solution.py:585
  61.0 4.7 %shard_map.59 = (f32[512,128]{1,0:T(8,128)}, f32[3,512,128]{2,1,0:T(8,128)}, f32[16,512,128]{2,1,0:T(8,128)}) custom-call(f32[7,512,128]{2,1,0:T(8,128)S(1)} %get-tuple-element.11.k_ref, f32[16,576,128]{2,1,0:T(8,128)S(1)} %get-tuple-element.12.c1, f32[2,16,64,128]{3,2,1,0:T(8,128)S(1)} %get-tuple-element.13.c1n, f32[512,128]{1,0:T(8,128)S(1)} %get-tuple-element.14.p, ...), custom_call_target="tpu_custom_call" | custom-call | tf_op jit(solution)/shard_map/pallas_call | solution.py:610
Async XLA Ops:
  0.6 2.2 %copy-start = (f32[16,16,8,512]{3,2,1,0:T(8,128)S(1)}, f32[16,16,8,512]{3,2,1,0:T(8,128)}, u32[]{:S(2)}) copy-start(f32[16,16,8,512]{3,2,1,0:T(8,128)} %param.5) | copy-start | bytes 12582916
  2.8 1.1 %copy-start.1 = (f32[3,16,8,512]{3,2,1,0:T(8,128)S(1)}, f32[3,16,8,512]{3,2,1,0:T(8,128)}, u32[]{:S(2)}) copy-start(f32[3,16,8,512]{3,2,1,0:T(8,128)} %param.3) | copy-start | bytes 2359300
  4.0 1.1 %copy-start.2 = (f32[3,16,8,512]{3,2,1,0:T(8,128)S(1)}, f32[3,16,8,512]{3,2,1,0:T(8,128)}, u32[]{:S(2)}) copy-start(f32[3,16,8,512]{3,2,1,0:T(8,128)} %param.4) | copy-start | bytes 2359300

commit v2 on v1

--- a/solution.py
+++ b/solution.py
@@ -309,7 +309,7 @@
         put_plane(v_s.at[0], i + 1, v)
         return acc + total(mul(rhs, v))
 
-    b0 = lax.fori_loop(0, PLANES, start_plane, zero)
+    b0 = lax.fori_loop(0, PLANES, start_plane, zero, unroll=True)
 
     def exchange(s):
         v = v_s.at[s]
@@ -349,7 +349,7 @@
         g00, g01, b1 = acc
         return g00 + total(mul(v, a)), g01 + total(mul(new, a)), b1 + total(mul(new, plane(rhs_s, i)))
 
-    g00, g01, b1 = lax.fori_loop(0, PLANES, first_plane, (zero, zero, zero))
+    g00, g01, b1 = lax.fori_loop(0, PLANES, first_plane, (zero, zero, zero), unroll=True)
     got = exchange(1)
     send_bulk(2)
     for arrive in got:
@@ -365,7 +365,7 @@
             g02 + total(mul(new, plane(a0_s, i))), b2 + total(mul(new, plane(rhs_s, i))),
         )
 
-    g11, g12, g02, b2 = lax.fori_loop(0, PLANES, second_plane, (zero,) * 4)
+    g11, g12, g02, b2 = lax.fori_loop(0, PLANES, second_plane, (zero,) * 4, unroll=True)
     got = exchange(2)
     send_bulk(3)
 
@@ -385,7 +385,7 @@
         v, a = image(2, i)
         return g22 + total(mul(v, a))
 
-    sums = sums + place(lax.fori_loop(0, PLANES, third_plane, zero), 8)
+    sums = sums + place(lax.fori_loop(0, PLANES, third_plane, zero, unroll=True), 8)
 
     pending = []
     for g, group in enumerate((group_n, group_w)):
@@ -426,7 +426,7 @@
         put_plane(pe, i, [q0 * vs[0][c] + q1 * vs[1][c] + q2 * vs[2][c] for c in range(CH)])
         return 0
 
-    lax.fori_loop(0, PLANES + 2, combine, 0)
+    lax.fori_loop(0, PLANES + 2, combine, 0, unroll=True)
     for side in range(2):
         for r in range(EDGE // 8):
             rows = pl.ds(r * 8, 8)
@@ -454,7 +454,7 @@
         put_plane(vz, i + 1, uz)
         return 0
 
-    lax.fori_loop(0, PLANES, velocity_plane, 0)
+    lax.fori_loop(0, PLANES, velocity_plane, 0, unroll=True)
 
     one = lambda i: pl.ds(i * PR, PR)
     got = [
@@ -518,20 +518,25 @@
             else:
                 uy, uyd = far, kedge[0, pl.ds(r * 8, 8), :]
             k = weights([ux], [uxd], [uy], [uyd], [uz], [packed_below_k(uz)])
-            k = [[m[0] * inside] for m in k]
-
-            def row_step(t, _, side=side, r=r, k=k):
-                ref = t_r1.at[side, t]
+            for m in range(7):
+                kn[side, m, pl.ds(r * 8, 8), :] = k[m][0] * inside
+
+    def row_step(t, _):
+        for side in range(2):
+            ref = t_r1.at[side, t]
+            for r in range(EDGE // 8):
+                rows = pl.ds(r * 8, 8)
                 c = ref[pl.ds(8 + r * 8, 8), :]
                 xu, xd = ref[pl.ds(12 + r * 8, 8), :], ref[pl.ds(4 + r * 8, 8), :]
-                far = t_r2[side, t, pl.ds(r * 8, 8), :]
-                near = t_send[0 if side == 0 else 3, t, pl.ds(r * 8, 8), :]
+                far = t_r2[side, t, rows, :]
+                near = t_send[0 if side == 0 else 3, t, rows, :]
                 yu, yd = (near, far) if side == 0 else (far, near)
+                k = [[kn[side, m, rows, :]] for m in range(7)]
                 out = apply_weights(k, [c], [xu], [xd], [yu], [yd], [packed_next_k(c)], [packed_below_k(c)])
-                c1n_o[side, t, pl.ds(r * 8, 8), :] = out[0]
-                return 0
-
-            lax.fori_loop(0, TR, row_step, 0, unroll=8)
+                c1n_o[side, t, rows, :] = out[0]
+        return 0
+
+    lax.fori_loop(0, TR, row_step, 0, unroll=2)
 
     for copy in pending:
         copy.wait_send()
@@ -598,7 +603,7 @@
             vm(2, 1, 128), vm(2, 31, 1, 128),
             vm(18 * PR, 128), vm(2, EDGE, 128),
             vm(19 * PR, 128), vm(18 * PR, 128), vm(18 * PR, 128), vm(16 + EDGE, 128), vm(EDGE, 128),
-            vm(2, 3 * EDGE + 8, 128), vm(2, 3 * EDGE + 8, 128), vm(7, 8, 128), vm(1, EDGE, 128),
+            vm(2, 3 * EDGE + 8, 128), vm(2, 3 * EDGE + 8, 128), vm(2, 7, EDGE, 128), vm(1, EDGE, 128),
             vm(TR, 20 * PR, 128), vm(4, TR, EDGE, 128), vm(2, TR, 16 + EDGE, 128), vm(2, TR, EDGE, 128),
             pltpu.SemaphoreType.DMA((7,)), pltpu.SemaphoreType.DMA((64,)), pltpu.SemaphoreType.DMA((64,)),
             pltpu.SemaphoreType.DMA((2, 31)), pltpu.SemaphoreType.DMA((2, 31)),
@@ -606,7 +611,7 @@
         compiler_params=pltpu.CompilerParams(
             collective_id=0, has_side_effects=True, vmem_limit_bytes=40 << 20
         ),
-    )(view(coefficients), view(predicted_velocity), view(tracers))
+    )(*[pltpu.with_memory_space_constraint(view(x), pltpu.HBM) for x in (coefficients, predicted_velocity, tracers)])
     p, vel, tr = pl.pallas_call(
         transport_kernel,
         out_shape=[shape(OWN, 128), shape(3, OWN, 128), shape(TR, OWN, 128)],

time: 65.9 us -> 50.1 us (0.76)
  Pallas kernels: 60.6 us -> 49.4 us
  local copies, waits for them, and re-layouts: 4.45 us -> 0 us
    pallas_call x1, Pallas kernels: 55.9 us -> 44.7 us  [body(): pl.pallas_call(pressure_kernel, out_shape=[shape(OWN, 128), shape(3, OWN,...]
    unnamed x6 -> x0, local copies, waits for them, and re-layouts: 4.45 us -> none
where the time goes in v2:
time: 50.1 us
  Pallas kernels  49.4 us (99%)
  between operations  0.64 us (1%)
    pallas_call x1, Pallas kernels, body(): pl.pallas_call(pressure_kernel, out_shape=[shape(OWN, 128), shape(3, OWN,...  44.7 us
    pallas_call x1, Pallas kernels, body(): pl.pallas_call(transport_kernel, out_shape=[shape(OWN, 128), shape(3, OWN...  4.68 us

profile of v2, /device:TPU:1, one launch (start us, length us, event | category | flops | bytes accessed | tf_op | source)
XLA Modules:
  0.0 50.1 jit_solution(4158357954247593088)
XLA Ops:
  0.6 44.7 %shard_map.58 = (f32[512,128]{1,0:T(8,128)S(1)}, f32[3,512,128]{2,1,0:T(8,128)S(1)}, f32[7,512,128]{2,1,0:T(8,128)S(1)}, f32[16,576,128]{2,1,0:T(8,128)S(1)}, f32[2,16,64,128]{3,2,1,0:T(8,128)S(1)}) custom-call(f32[3,512,128]{2,1,0:T(8,128)} %bitcast.31, f32[3,512,128]{2,1,0:T(8,128)} %bitcast.32, f32[16,512,128]{2,1,0:T(8,128)} %bitcast.30), custom_call_target="tpu_custom_call" | custom-call | tf_op jit(solution)/shard_map/pallas_call | solution.py:590
  45.4 4.7 %shard_map.59 = (f32[512,128]{1,0:T(8,128)}, f32[3,512,128]{2,1,0:T(8,128)}, f32[16,512,128]{2,1,0:T(8,128)}) custom-call(f32[7,512,128]{2,1,0:T(8,128)S(1)} %get-tuple-element.11.k_ref, f32[16,576,128]{2,1,0:T(8,128)S(1)} %get-tuple-element.12.c1, f32[2,16,64,128]{3,2,1,0:T(8,128)S(1)} %get-tuple-element.13.c1n, f32[512,128]{1,0:T(8,128)S(1)} %get-tuple-element.14.p, ...), custom_call_target="tpu_custom_call" | custom-call | tf_op jit(solution)/shard_map/pallas_call | solution.py:615

commit v3 on v2

--- a/solution.py
+++ b/solution.py
@@ -22,6 +22,9 @@
 NWIDE = 32
 NNARROW = 8
 SHIFT = 1.0
+N_PIL, N_CY, N_PY = 2 * EDGE, 2 * EDGE + 8, 3 * EDGE + 8
+NROWS = 4 * EDGE + 8
+CORNERS = ((1, 1), (-1, 1), (1, -1), (-1, -1))
 
 
 def lane_id():
@@ -126,20 +129,26 @@
     return out
 
 
-def transport_plane(k, field, i, low_ref, high_ref, r):
-    c = plane(field, i)
-    xu, xd = plane(field, i + 1), plane(field, i - 1)
-    yu, yd = next_j(c, edge_rows(high_ref, r)), below_j(c, edge_rows(low_ref, r))
-    return apply_weights(k, c, xu, xd, yu, yd, next_k(c), below_k(c))
+def planes_of(field, at, out, to, k_ref, k_at, low_ref, high_ref, r, which):
+    xd = plane(field, which[0] + at - 1)
+    c = plane(field, which[0] + at)
+    for i in which:
+        xu = plane(field, i + at + 1)
+        k = [plane(k_ref.at[m], i + k_at) for m in range(7)]
+        low, high = edge_rows(low_ref, r + i * CH), edge_rows(high_ref, r + i * CH)
+        put_plane(
+            out, i + to, apply_weights(k, c, xu, xd, next_j(c, high), below_j(c, low), next_k(c), below_k(c))
+        )
+        xd, c = c, xu
 
 
 def pressure_kernel(
     co_h, pv_h, tr_h,
     p_o, vel_o, k_o, c1_o, c1n_o,
-    cxe, cy, cz, pxe, py, pz, low_n, e1_send,
-    rhs_s, inv_s, a0_s, v_s, vn_send, vn_recv,
+    cxe, cy, cz, pxe, py, pz, part, w_recv, w_pil_send, w_pil, n_send, n_recv, d_send, d_recv,
+    rhs_s, inv_s, w_inv, n_inv, a0_s, a1_s, v_s, vn_send, vn_recv, vc_recv, wb_recv, nb_send, nb_recv,
     red_send, red_recv,
-    pe, pn, vx, vy, vz, vyl, pn0, e5_send, e5_recv, kn, kedge,
+    pe, pn, vx, vy, vz, vyl, pn0, e5_send, e5_recv, kn, kedge, k_s,
     te, t_send, t_r1, t_r2,
     lsem, ssem, rsem, red_ss, red_rs,
 ):
@@ -201,27 +210,34 @@
 
         return arrive
 
-    def blank(dst, way):
+    def blank(dst, way, value=0.0):
         @pl.when(jnp.logical_not(has[way]))
         def _():
-            dst[...] = jnp.zeros(dst.shape, F32)
+            dst[...] = jnp.full(dst.shape, value, F32)
+
+    low_cy, low_py = n_recv.at[0, pl.ds(N_CY, EDGE)], n_recv.at[0, pl.ds(N_PY, EDGE)]
 
     for ref, dst in ((cxe, pl.ds(0, PR)), (pxe, pl.ds(0, PR))):
         blank(ref.at[dst], (-1, 0))
-    blank(low_n.at[0], (0, -1))
-    blank(low_n.at[1], (0, -1))
-    for s in range(3):
-        blank(v_s.at[s, pl.ds(0, PR)], (-1, 0))
-        blank(v_s.at[s, pl.ds(17 * PR, PR)], (1, 0))
-        blank(vn_recv.at[s, 0], (0, -1))
-        blank(vn_recv.at[s, 1], (0, 1))
+    for side, sign in ((0, -1), (1, 1)):
+        blank(w_recv.at[side, 0], (sign, 0))
+        blank(w_recv.at[side, 1], (sign, 0), 1.0)
+        blank(w_pil.at[side], (sign, 0))
+        blank(n_recv.at[side], (0, sign))
+        blank(n_recv.at[side, pl.ds(EDGE, EDGE)], (0, sign), 1.0)
+        blank(v_s.at[1, pl.ds(side * 17 * PR, PR)], (sign, 0))
+        blank(vn_recv.at[1, side], (0, sign))
+        blank(wb_recv.at[side], (sign, 0))
+        blank(nb_recv.at[side], (0, sign))
+        blank(e5_recv.at[side], (0, sign))
+    for q, way in enumerate(CORNERS):
+        blank(d_recv.at[q], way)
+        blank(vc_recv.at[q], way)
     for ref, low, high in ((vx, 0, 18), (vy, 0, 17), (vz, 0, 17)):
         blank(ref.at[pl.ds(low * PR, PR)], (-1, 0))
         blank(ref.at[pl.ds(high * PR, PR)], (1, 0))
     blank(vyl.at[pl.ds(0, 8)], (-1, 0))
     blank(vyl.at[pl.ds(8 + EDGE, 8)], (1, 0))
-    blank(e5_recv.at[0], (0, -1))
-    blank(e5_recv.at[1], (0, 1))
 
     def blank_tracers(t, _):
         blank(te.at[t, pl.ds(0, 2 * PR)], (-1, 0))
@@ -235,41 +251,83 @@
 
     lax.fori_loop(0, TR, blank_tracers, 0)
 
-    pl.semaphore_wait(barrier, len(peers))
-
     def pack(src, base, j):
         return src[pl.ds(base + j, EDGE, stride=8), :]
 
+    def pillar(src, base, i, j):
+        return src[pl.ds(base + i * PR + j, CH, stride=8), :]
+
+    zero = jnp.zeros((8, 128), F32)
+    first_j, last_j = sub_id() == 0, sub_id() == 7
+
+    for copy in loads[:6]:
+        copy.wait()
+    for i in range(PLANES):
+        cxu, cyu, czu = plane(cxe, i + 1), plane(cy, i), plane(cz, i)
+        diag = add(add(cxu, add(cyu, below_j(cyu, [zero] * CH))), add(czu, below_k(czu)))
+        pxu, pyu, pzu = plane(pxe, i + 1), plane(py, i), plane(pz, i)
+        d = add(add(pxu, sub(pyu, below_j(pyu, [zero] * CH))), sub(pzu, below_k(pzu)))
+        if i:
+            diag = add(diag, plane(cxe, i))
+            d = sub(d, plane(pxe, i))
+        put_plane(part.at[0], i, [-x for x in d])
+        put_plane(part.at[1], i, diag)
+    for side, i, j in ((0, 0, 0), (1, PLANES - 1, 7)):
+        n_send[side, pl.ds(0, EDGE)] = pack(part.at[0], 0, j)
+        n_send[side, pl.ds(EDGE, EDGE)] = pack(part.at[1], 0, j)
+        n_send[side, pl.ds(N_PIL, 8)] = zero
+        n_send[side, pl.ds(N_PIL, CH)] = pillar(cxe, PR, PLANES - 1, j)
+        w_pil_send[side] = zero
+        w_pil_send[side, pl.ds(0, CH)] = pillar(cy, 0, i, 7)
+    n_send[1, pl.ds(N_CY, EDGE)] = pack(cy, 0, 7)
+    n_send[1, pl.ds(N_PY, EDGE)] = pack(py, 0, 7)
+    for q, (a, b) in enumerate(CORNERS):
+        i, j = (PLANES - 1 if a > 0 else 0), (7 if b > 0 else 0)
+        for m, (ref, base) in enumerate(((cxe, PR), (pxe, PR), (cy, 0), (py, 0))):
+            d_send[q, pl.ds(m * CH, CH)] = pillar(ref, base, i, j)
+
+    pl.semaphore_wait(barrier, len(peers))
+
     got = [
-        message(co_h.at[0, pl.ds(OWN - PR, PR)], cxe.at[pl.ds(0, PR)], (1, 0)),
-        message(pv_h.at[0, pl.ds(OWN - PR, PR)], pxe.at[pl.ds(0, PR)], (1, 0)),
+        message(d_send.at[q], d_recv.at[3 - q], way) for q, way in enumerate(CORNERS) if way != (-1, -1)
     ]
-    loads[0].wait()
-    e1_send[0] = pack(cy, 0, 7)
-    loads[1].wait()
-    e1_send[1] = pack(py, 0, 7)
-    got.append(message(e1_send, low_n, (0, 1)))
+    last, front = pl.ds(OWN - PR, PR), pl.ds(0, PR)
+    n_low = pl.ds(0, N_CY)
+    got += [
+        message(part.at[:, last], w_recv.at[0], (1, 0)),
+        message(part.at[:, front], w_recv.at[1], (-1, 0)),
+        message(n_send.at[1], n_recv.at[0], (0, 1)),
+        message(n_send.at[0, n_low], n_recv.at[1, n_low], (0, -1)),
+        message(cxe.at[pl.ds(OWN, PR)], cxe.at[front], (1, 0)),
+        message(pxe.at[pl.ds(OWN, PR)], pxe.at[front], (1, 0)),
+        message(w_pil_send.at[1], w_pil.at[0], (1, 0)),
+        message(w_pil_send.at[0], w_pil.at[1], (-1, 0)),
+    ]
 
     bulk = []
 
-    def send_bulk(chunk):
-        t0 = chunk * PER
-
+    def pack_tracers():
         def rows(t, _):
             for slot, j in enumerate((0, 1, 6, 7)):
                 t_send[slot, t] = te[t, pl.ds(2 * PR + j, EDGE, stride=8), :]
             return 0
 
-        lax.fori_loop(t0, t0 + PER, rows, 0)
-        ts = pl.ds(t0, PER)
-        main = pl.ds(8, EDGE)
+        lax.fori_loop(0, TR, rows, 0)
+
+    def send_rows(chunk):
+        ts, main = pl.ds(chunk * PER, PER), pl.ds(8, EDGE)
         bulk.extend([
             message(t_send.at[3, ts], t_r1.at[0, ts, main], (0, 1)),
             message(t_send.at[0, ts], t_r1.at[1, ts, main], (0, -1)),
+            message(t_send.at[2, ts], t_r2.at[0, ts], (0, 1)),
+            message(t_send.at[1, ts], t_r2.at[1, ts], (0, -1)),
+        ])
+
+    def send_planes(chunk):
+        ts = pl.ds(chunk * PER, PER)
+        bulk.extend([
             message(te.at[ts, pl.ds(16 * PR, 2 * PR)], te.at[ts, pl.ds(0, 2 * PR)], (1, 0)),
             message(te.at[ts, pl.ds(2 * PR, 2 * PR)], te.at[ts, pl.ds(18 * PR, 2 * PR)], (-1, 0)),
-            message(t_send.at[2, ts], t_r2.at[0, ts], (0, 1)),
-            message(t_send.at[1, ts], t_r2.at[1, ts], (0, -1)),
         ])
 
     def send_corners():
@@ -283,44 +341,52 @@
         ])
 
     loads[6].wait()
-    send_bulk(0)
-    for copy in loads[2:6]:
-        copy.wait()
+    pack_tracers()
+    send_rows(0)
+    send_rows(1)
+    send_planes(0)
+    send_planes(1)
     for arrive in got:
         arrive()
 
-    zero = jnp.zeros((8, 128), F32)
-
-    def start_plane(i, acc):
-        cxu, cxd = plane(cxe, i + 1), plane(cxe, i)
-        cyu, czu = plane(cy, i), plane(cz, i)
-        cyd = below_j(cyu, edge_rows(low_n.at[0], i * CH))
-        czd = below_k(czu)
-        diag = add(add(add(cxu, cxd), add(cyu, cyd)), add(czu, czd))
-        pyu, pzu = plane(py, i), plane(pz, i)
-        pyd = below_j(pyu, edge_rows(low_n.at[1], i * CH))
-        d = sub(plane(pxe, i + 1), plane(pxe, i))
-        d = add(add(d, sub(pyu, pyd)), sub(pzu, below_k(pzu)))
-        rhs = [-x for x in d]
+    corner = {way: d_recv.at[q] for q, way in enumerate(CORNERS)}
+    pick_low = lambda rows: [jnp.where(first_j, x, 0.0) for x in rows]
+    pick_high = lambda rows: [jnp.where(last_j, x, 0.0) for x in rows]
+
+    b0 = zero
+    for i in range(PLANES):
+        rhs = add(plane(part.at[0], i), pick_low(edge_rows(low_py, i * CH)))
+        diag = add(plane(part.at[1], i), pick_low(edge_rows(low_cy, i * CH)))
+        if i == 0:
+            rhs, diag = add(rhs, plane(pxe, 0)), add(diag, plane(cxe, 0))
         inv = [1.0 / x for x in diag]
         v = mul(rhs, inv)
         put_plane(rhs_s, i, rhs)
         put_plane(inv_s, i, inv)
         put_plane(v_s.at[0], i + 1, v)
-        return acc + total(mul(rhs, v))
-
-    b0 = lax.fori_loop(0, PLANES, start_plane, zero, unroll=True)
-
-    def exchange(s):
-        v = v_s.at[s]
-        for slot, j in ((0, 0), (1, 7)):
-            vn_send[s, slot] = pack(v, PR, j)
-        return [
-            message(v.at[pl.ds(PR * 16, PR)], v.at[pl.ds(0, PR)], (1, 0)),
-            message(v.at[pl.ds(PR, PR)], v.at[pl.ds(PR * 17, PR)], (-1, 0)),
-            message(vn_send.at[s, 1], vn_recv.at[s, 0], (0, 1)),
-            message(vn_send.at[s, 0], vn_recv.at[s, 1], (0, -1)),
-        ]
+        b0 = b0 + total(mul(rhs, v))
+    for side, sign in ((0, -1), (1, 1)):
+        inside = jnp.where(has[(sign, 0)], 1.0, 0.0)
+        ref = corner[(sign, -1)]
+        rhs = add(plane(w_recv.at[side, 0], 0), pick_low(edge_rows(ref, 3 * CH)))
+        diag = add(plane(w_recv.at[side, 1], 0), pick_low(edge_rows(ref, 2 * CH)))
+        if side:
+            rhs, diag = add(rhs, plane(pxe, PLANES)), add(diag, plane(cxe, PLANES))
+        inv = [inside / x for x in diag]
+        put_plane(w_inv.at[side], 0, inv)
+        put_plane(v_s.at[0], 17 * side, mul(rhs, inv))
+    for side, sign in ((0, -1), (1, 1)):
+        inside = jnp.where(has[(0, sign)], 1.0, 0.0)
+        ref = corner[(-1, sign)]
+        head, mid = pl.ds(0, CH), pl.ds(EDGE, CH)
+        n_recv[side, head] = n_recv[side, head] + ref[pl.ds(CH, CH), :]
+        n_recv[side, mid] = n_recv[side, mid] + ref[pl.ds(0, CH), :]
+        rhs, diag = n_recv[side, pl.ds(0, EDGE)], n_recv[side, pl.ds(EDGE, EDGE)]
+        if side:
+            rhs, diag = rhs + n_send[1, pl.ds(N_PY, EDGE)], diag + n_send[1, pl.ds(N_CY, EDGE)]
+        inv = inside / diag
+        n_inv[side] = inv
+        vn_recv[0, side] = rhs * inv
 
     def image(s, i):
         v_ref = v_s.at[s]
@@ -330,44 +396,57 @@
         fxd = mul(plane(cxe, i), sub(v, vd))
         low, high = edge_rows(vn_recv.at[s, 0], i * CH), edge_rows(vn_recv.at[s, 1], i * CH)
         fy = mul(plane(cy, i), sub(next_j(v, high), v))
-        edge = mul(edge_rows(low_n.at[0], i * CH), sub(v, low))
+        edge = mul(edge_rows(low_cy, i * CH), sub(v, low))
         fyd = below_j(fy, edge)
         fz = mul(plane(cz, i), sub(next_k(v), v))
         a = add(add(sub(fxd, fx), sub(fyd, fy)), sub(below_k(fz), fz))
         return v, a
 
-    got = exchange(0)
-    send_bulk(1)
-    for arrive in got:
-        arrive()
-
-    def first_plane(i, acc):
+    g00 = g01 = b1 = zero
+    for i in range(PLANES):
         v, a = image(0, i)
         put_plane(a0_s, i, a)
         new = sub(mul(a, plane(inv_s, i)), [x * SHIFT for x in v])
         put_plane(v_s.at[1], i + 1, new)
-        g00, g01, b1 = acc
-        return g00 + total(mul(v, a)), g01 + total(mul(new, a)), b1 + total(mul(new, plane(rhs_s, i)))
-
-    g00, g01, b1 = lax.fori_loop(0, PLANES, first_plane, (zero, zero, zero), unroll=True)
-    got = exchange(1)
-    send_bulk(2)
-    for arrive in got:
-        arrive()
-
-    def second_plane(i, acc):
-        v, a = image(1, i)
-        new = sub(mul(a, plane(inv_s, i)), [x * SHIFT for x in v])
-        put_plane(v_s.at[2], i + 1, new)
-        g11, g12, g02, b2 = acc
-        return (
-            g11 + total(mul(v, a)), g12 + total(mul(new, a)),
-            g02 + total(mul(new, plane(a0_s, i))), b2 + total(mul(new, plane(rhs_s, i))),
-        )
-
-    g11, g12, g02, b2 = lax.fori_loop(0, PLANES, second_plane, (zero,) * 4, unroll=True)
-    got = exchange(2)
-    send_bulk(3)
+        g00, g01, b1 = g00 + total(mul(v, a)), g01 + total(mul(new, a)), b1 + total(mul(new, plane(rhs_s, i)))
+
+    v1 = v_s.at[1]
+    for slot, j in ((0, 0), (1, 7)):
+        vn_send[1, slot] = pack(v1, PR, j)
+    got = [
+        message(vn_send.at[1, 1 if b > 0 else 0, pl.ds(EDGE - 8 if a > 0 else 0, 8)], vc_recv.at[3 - q], (a, b))
+        for q, (a, b) in enumerate(CORNERS)
+    ]
+    got += [
+        message(v1.at[pl.ds(PR * 16, PR)], v1.at[pl.ds(0, PR)], (1, 0)),
+        message(v1.at[pl.ds(PR, PR)], v1.at[pl.ds(PR * 17, PR)], (-1, 0)),
+        message(vn_send.at[1, 1], vn_recv.at[1, 0], (0, 1)),
+        message(vn_send.at[1, 0], vn_recv.at[1, 1], (0, -1)),
+    ]
+    fxd = None
+    for i in range(PLANES):
+        v = plane(v1, i + 1)
+        fy = [jnp.where(last_j, 0.0, x) for x in mul(plane(cy, i), sub(next_j(v, v), v))]
+        fz = mul(plane(cz, i), sub(next_k(v), v))
+        a = add(sub(below_j(fy, [zero] * CH), fy), sub(below_k(fz), fz))
+        if i:
+            a = add(a, fxd)
+        if i < PLANES - 1:
+            fxd = mul(plane(cxe, i + 1), sub(plane(v1, i + 2), v))
+            a = sub(a, fxd)
+        put_plane(a1_s, i, a)
+    nb_send[0] = pack(a1_s, 0, 0)
+    nb_send[1] = pack(a1_s, 0, 7)
+    got += [
+        message(a1_s.at[last], wb_recv.at[0], (1, 0)),
+        message(a1_s.at[front], wb_recv.at[1], (-1, 0)),
+        message(nb_send.at[1], nb_recv.at[0], (0, 1)),
+        message(nb_send.at[0], nb_recv.at[1], (0, -1)),
+    ]
+    send_rows(2)
+    send_planes(2)
+    send_planes(3)
+    send_corners()
 
     lane = lax.broadcasted_iota(jnp.int32, (1, 128), 1)
 
@@ -376,16 +455,59 @@
         return jnp.where(lane == m, s, 0.0)
 
     sums = jnp.zeros((1, 128), F32)
-    for m, x in enumerate((b0, b1, b2, g00, g01, g02, g11, g12)):
+    for m, x in ((0, b0), (1, b1), (3, g00), (4, g01)):
         sums = sums + place(x, m)
     for arrive in got:
         arrive()
 
-    def third_plane(i, g22):
+    g11 = g12 = g02 = b2 = zero
+    for i in range(PLANES):
+        v, a = plane(v1, i + 1), plane(a1_s, i)
+        low, high = edge_rows(vn_recv.at[1, 0], i * CH), edge_rows(vn_recv.at[1, 1], i * CH)
+        a = add(a, pick_low(mul(edge_rows(low_cy, i * CH), sub(v, low))))
+        a = sub(a, pick_high(mul(plane(cy, i), sub(high, v))))
+        if i == 0:
+            a = add(a, mul(plane(cxe, 0), sub(v, plane(v1, 0))))
+        if i == PLANES - 1:
+            a = sub(a, mul(plane(cxe, PLANES), sub(plane(v1, PLANES + 1), v)))
+        new = sub(mul(a, plane(inv_s, i)), [x * SHIFT for x in v])
+        put_plane(v_s.at[2], i + 1, new)
+        g11, g12 = g11 + total(mul(v, a)), g12 + total(mul(new, a))
+        g02, b2 = g02 + total(mul(new, plane(a0_s, i))), b2 + total(mul(new, plane(rhs_s, i)))
+
+    seen = {way: (vc_recv.at[q], CH if way[0] < 0 else 0) for q, way in enumerate(CORNERS)}
+    for side, sign in ((0, -1), (1, 1)):
+        v = plane(v1, 17 * side)
+        a = plane(wb_recv.at[side], 0)
+        if side == 0:
+            a = sub(a, mul(plane(cxe, 0), sub(plane(v1, 1), v)))
+        else:
+            a = add(a, mul(plane(cxe, PLANES), sub(v, plane(v1, PLANES))))
+        low, high = edge_rows(*seen[(sign, -1)]), edge_rows(*seen[(sign, 1)])
+        a = add(a, pick_low(mul(edge_rows(corner[(sign, -1)], 2 * CH), sub(v, low))))
+        a = sub(a, pick_high(mul(edge_rows(w_pil.at[side], 0), sub(high, v))))
+        new = sub(mul(a, plane(w_inv.at[side], 0)), [x * SHIFT for x in v])
+        put_plane(v_s.at[2], 17 * side, new)
+    for side, sign in ((0, -1), (1, 1)):
+        head, tail = pl.ds(0, CH), pl.ds(EDGE - CH, CH)
+        cell = lambda way: seen[way][0][pl.ds(seen[way][1], CH), :]
+        vh, vt = vn_recv[1, side, head], vn_recv[1, side, tail]
+        ch, ct = corner[(-1, sign)][pl.ds(0, CH), :], n_recv[side, pl.ds(N_PIL, CH)]
+        nb_recv[side, head] = nb_recv[side, head] + ch * (vh - cell((-1, sign)))
+        nb_recv[side, tail] = nb_recv[side, tail] - ct * (cell((1, sign)) - vt)
+        v, near = vn_recv[1, side], vn_send[1, side]
+        if side == 0:
+            a = nb_recv[side] - low_cy[...] * (near - v)
+        else:
+            a = nb_recv[side] + n_send[1, pl.ds(N_CY, EDGE)] * (v - near)
+        vn_recv[2, side] = a * n_inv[side] - v * SHIFT
+
+    g22 = zero
+    for i in range(PLANES):
         v, a = image(2, i)
-        return g22 + total(mul(v, a))
-
-    sums = sums + place(lax.fori_loop(0, PLANES, third_plane, zero, unroll=True), 8)
+        g22 = g22 + total(mul(v, a))
+    for m, x in ((2, b2), (5, g02), (6, g11), (7, g12), (8, g22)):
+        sums = sums + place(x, m)
 
     pending = []
     for g, group in enumerate((group_n, group_w)):
@@ -399,8 +521,8 @@
             )
             copy.start()
             copies.append(copy)
-        if g == 0:
-            send_corners()
+        if g == 1:
+            send_rows(3)
         for copy in copies:
             copy.wait_recv()
         sums = sums + jnp.sum(red_recv[g, 0 : len(group)], axis=0)
@@ -439,7 +561,7 @@
         put_plane(vx, 1, sub(plane(pxe, 0), mul(plane(cxe, 0), sub(p1, p0))))
 
     low_x()
-    vyl[pl.ds(8, EDGE), :] = low_n[1] - low_n[0] * (pack(pe, PR, 0) - pn[0])
+    vyl[pl.ds(8, EDGE), :] = low_py[...] - low_cy[...] * (pack(pe, PR, 0) - pn[0])
 
     def velocity_plane(i, _):
         p = plane(pe, i + 1)
@@ -484,26 +606,33 @@
         uyd = below_j(uy, edge_rows(vyl, 8 + i * CH))
         return weights(plane(vx, i + 2), plane(vx, i + 1), uy, uyd, uz, below_k(uz))
 
-    def step_plane(i, k):
-        for t in range(TR):
-            out = transport_plane(k, te.at[t], i + 2, t_r1.at[0, t], t_r1.at[1, t], 8 + i * CH)
-            put_plane(c1_o.at[t], i + 1, out)
-
-    def own_plane(i, _):
+    def put_weights(i, inside=None):
         k = plane_weights(i)
         for m in range(7):
-            put_plane(k_o.at[m], i, k[m])
-        step_plane(i, k)
+            put_plane(k_s.at[m], i + 1, k[m] if inside is None else [x * inside for x in k[m]])
+            if inside is None:
+                put_plane(k_o.at[m], i, k[m])
+
+    for i in range(PLANES):
+        put_weights(i)
+
+    def own_planes(t, _):
+        planes_of(te.at[t], 2, c1_o.at[t], 1, k_s, 1, t_r1.at[0, t], t_r1.at[1, t], 8, range(PLANES))
         return 0
 
-    lax.fori_loop(0, PLANES, own_plane, 0)
+    lax.fori_loop(0, TR, own_planes, 0, unroll=2)
     for arrive in got:
         arrive()
 
     for i, way in ((-1, (-1, 0)), (PLANES, (1, 0))):
-        inside = jnp.where(has[way], 1.0, 0.0)
-        k = [[x * inside for x in m] for m in plane_weights(i)]
-        step_plane(i, k)
+        put_weights(i, jnp.where(has[way], 1.0, 0.0))
+
+    def beside(t, _):
+        for i in (-1, PLANES):
+            planes_of(te.at[t], 2, c1_o.at[t], 1, k_s, 1, t_r1.at[0, t], t_r1.at[1, t], 8, [i])
+        return 0
+
+    lax.fori_loop(0, TR, beside, 0, unroll=4)
 
     kedge[0] = pack(vy, PR, 7)
     for side, way in ((0, (0, -1)), (1, (0, 1))):
@@ -550,22 +679,10 @@
     first = [pltpu.make_async_copy(p, p_h, sem.at[0]), pltpu.make_async_copy(vel, vel_h, sem.at[1])]
     for copy in first:
         copy.start()
-    copies = []
-    parts = 4
-    for part in range(parts):
-
-        def own_plane(i, _):
-            k = [plane(k_ref.at[m], i) for m in range(7)]
-            for t in range(TR):
-                put_plane(out.at[t], i, transport_plane(k, c1.at[t], i + 1, c1n.at[0, t], c1n.at[1, t], i * CH))
-            return 0
-
-        each = PLANES // parts
-        lax.fori_loop(part * each, (part + 1) * each, own_plane, 0)
-        rows = pl.ds(part * each * PR, each * PR)
-        copy = pltpu.make_async_copy(out.at[:, rows], tr_h.at[:, rows], sem.at[2 + part])
-        copy.start()
-        copies.append(copy)
+    copies = [pltpu.make_async_copy(out.at[t], tr_h.at[t], sem.at[2 + t]) for t in range(TR)]
+    for t in range(TR):
+        planes_of(c1.at[t], 1, out.at[t], 0, k_ref, 0, c1n.at[0, t], c1n.at[1, t], 0, range(PLANES))
+        copies[t].start()
     for copy in first + copies:
         copy.wait()
 
@@ -597,15 +714,17 @@
         out_specs=[vmem] * 5,
         scratch_shapes=[
             vm(OWN + PR, 128), vm(OWN, 128), vm(OWN, 128), vm(OWN + PR, 128), vm(OWN, 128), vm(OWN, 128),
-            vm(2, EDGE, 128), vm(2, EDGE, 128),
-            vm(OWN, 128), vm(OWN, 128), vm(OWN, 128), vm(3, 18 * PR, 128),
-            vm(3, 2, EDGE, 128), vm(3, 2, EDGE, 128),
+            vm(2, OWN, 128), vm(2, 2, PR, 128), vm(2, 8, 128), vm(2, 8, 128),
+            vm(2, NROWS, 128), vm(2, NROWS, 128), vm(4, 16, 128), vm(4, 16, 128),
+            vm(OWN, 128), vm(OWN, 128), vm(2, PR, 128), vm(2, EDGE, 128), vm(OWN, 128), vm(OWN, 128),
+            vm(3, 18 * PR, 128), vm(3, 2, EDGE, 128), vm(3, 2, EDGE, 128), vm(4, 8, 128),
+            vm(2, PR, 128), vm(2, EDGE, 128), vm(2, EDGE, 128),
             vm(2, 1, 128), vm(2, 31, 1, 128),
             vm(18 * PR, 128), vm(2, EDGE, 128),
             vm(19 * PR, 128), vm(18 * PR, 128), vm(18 * PR, 128), vm(16 + EDGE, 128), vm(EDGE, 128),
-            vm(2, 3 * EDGE + 8, 128), vm(2, 3 * EDGE + 8, 128), vm(2, 7, EDGE, 128), vm(1, EDGE, 128),
+            vm(2, 3 * EDGE + 8, 128), vm(2, 3 * EDGE + 8, 128), vm(2, 7, EDGE, 128), vm(1, EDGE, 128), vm(7, 18 * PR, 128),
             vm(TR, 20 * PR, 128), vm(4, TR, EDGE, 128), vm(2, TR, 16 + EDGE, 128), vm(2, TR, EDGE, 128),
-            pltpu.SemaphoreType.DMA((7,)), pltpu.SemaphoreType.DMA((64,)), pltpu.SemaphoreType.DMA((64,)),
+            pltpu.SemaphoreType.DMA((7,)), pltpu.SemaphoreType.DMA((72,)), pltpu.SemaphoreType.DMA((72,)),
             pltpu.SemaphoreType.DMA((2, 31)), pltpu.SemaphoreType.DMA((2, 31)),
         ],
         compiler_params=pltpu.CompilerParams(
@@ -617,7 +736,7 @@
         out_shape=[shape(OWN, 128), shape(3, OWN, 128), shape(TR, OWN, 128)],
         in_specs=[vmem] * 5,
         out_specs=[hbm] * 3,
-        scratch_shapes=[vm(TR, OWN, 128), pltpu.SemaphoreType.DMA((6,))],
+        scratch_shapes=[vm(TR, OWN, 128), pltpu.SemaphoreType.DMA((2 + TR,))],
         compiler_params=pltpu.CompilerParams(vmem_limit_bytes=40 << 20),
     )(k, c1, c1n, p, vel)
     return unview(p), unview(vel), unview(tr)

time: 50.1 us -> 46.1 us (0.920)
  Pallas kernels: 49.4 us -> 45.4 us
    pallas_call x1, Pallas kernels: 44.7 us -> 41.8 us  [body(): pl.pallas_call(pressure_kernel, out_shape=[shape(OWN, 128), shape(3, OWN,...]
    pallas_call x1, Pallas kernels: 4.68 us -> 3.62 us  [body(): pl.pallas_call(transport_kernel, out_shape=[shape(OWN, 128), shape(3, OWN...]
where the time goes in v3:
time: 46.1 us; the launch traced here: 46 us
  Pallas kernels  45.4 us (98%)
  between operations  0.64 us (1%)
    pallas_call x1, Pallas kernels, body(): pl.pallas_call(pressure_kernel, out_shape=[shape(OWN, 128), shape(3, OWN,...  41.8 us
    pallas_call x1, Pallas kernels, body(): pl.pallas_call(transport_kernel, out_shape=[shape(OWN, 128), shape(3, OWN...  3.62 us

profile of v3, /device:TPU:1, one launch (start us, length us, event | category | flops | bytes accessed | tf_op | source)
XLA Modules:
  0.0 46.0 jit_solution(15529124537609498394)
XLA Ops:
  0.6 41.8 %shard_map.58 = (f32[512,128]{1,0:T(8,128)S(1)}, f32[3,512,128]{2,1,0:T(8,128)S(1)}, f32[7,512,128]{2,1,0:T(8,128)S(1)}, f32[16,576,128]{2,1,0:T(8,128)S(1)}, f32[2,16,64,128]{3,2,1,0:T(8,128)S(1)}) custom-call(f32[3,512,128]{2,1,0:T(8,128)} %bitcast.31, f32[3,512,128]{2,1,0:T(8,128)} %bitcast.32, f32[16,512,128]{2,1,0:T(8,128)} %bitcast.30), custom_call_target="tpu_custom_call" | custom-call | tf_op jit(solution)/shard_map/pallas_call | solution.py:707
  42.4 3.6 %shard_map.59 = (f32[512,128]{1,0:T(8,128)}, f32[3,512,128]{2,1,0:T(8,128)}, f32[16,512,128]{2,1,0:T(8,128)}) custom-call(f32[7,512,128]{2,1,0:T(8,128)S(1)} %get-tuple-element.11.k_ref, f32[16,576,128]{2,1,0:T(8,128)S(1)} %get-tuple-element.12.c1, f32[2,16,64,128]{3,2,1,0:T(8,128)S(1)} %get-tuple-element.13.c1n, f32[512,128]{1,0:T(8,128)S(1)} %get-tuple-element.14.p, ...), custom_call_target="tpu_custom_call" | custom-call | tf_op jit(solution)/shard_map/pallas_call | solution.py:734

commit v4 on v3

--- a/solution.py
+++ b/solution.py
@@ -304,7 +304,8 @@
         message(w_pil_send.at[0], w_pil.at[1], (-1, 0)),
     ]
 
-    bulk = []
+    bulk = [[] for _ in range(CHUNKS)]
+    late = []
 
     def pack_tracers():
         def rows(t, _):
@@ -316,16 +317,18 @@
 
     def send_rows(chunk):
         ts, main = pl.ds(chunk * PER, PER), pl.ds(8, EDGE)
-        bulk.extend([
+        bulk[chunk].extend([
             message(t_send.at[3, ts], t_r1.at[0, ts, main], (0, 1)),
             message(t_send.at[0, ts], t_r1.at[1, ts, main], (0, -1)),
+        ])
+        late.extend([
             message(t_send.at[2, ts], t_r2.at[0, ts], (0, 1)),
             message(t_send.at[1, ts], t_r2.at[1, ts], (0, -1)),
         ])
 
     def send_planes(chunk):
         ts = pl.ds(chunk * PER, PER)
-        bulk.extend([
+        bulk[chunk].extend([
             message(te.at[ts, pl.ds(16 * PR, 2 * PR)], te.at[ts, pl.ds(0, 2 * PR)], (1, 0)),
             message(te.at[ts, pl.ds(2 * PR, 2 * PR)], te.at[ts, pl.ds(18 * PR, 2 * PR)], (-1, 0)),
         ])
@@ -333,7 +336,7 @@
     def send_corners():
         low, high = pl.ds(0, 8), pl.ds(8 + EDGE, 8)
         first, last = pl.ds(0, 8), pl.ds(EDGE - 8, 8)
-        bulk.extend([
+        late.extend([
             message(t_send.at[3, :, last], t_r1.at[0, :, low], (1, 1)),
             message(t_send.at[3, :, first], t_r1.at[0, :, high], (-1, 1)),
             message(t_send.at[0, :, last], t_r1.at[1, :, low], (1, -1)),
@@ -445,8 +448,6 @@
     ]
     send_rows(2)
     send_planes(2)
-    send_planes(3)
-    send_corners()
 
     lane = lax.broadcasted_iota(jnp.int32, (1, 128), 1)
 
@@ -521,8 +522,12 @@
             )
             copy.start()
             copies.append(copy)
+        if g == 0:
+            pass
         if g == 1:
             send_rows(3)
+            send_planes(3)
+            send_corners()
         for copy in copies:
             copy.wait_recv()
         sums = sums + jnp.sum(red_recv[g, 0 : len(group)], axis=0)
@@ -598,9 +603,6 @@
     got.append(message(e5_send.at[1], e5_recv.at[0], (0, 1)))
     got.append(message(e5_send.at[0], e5_recv.at[1], (0, -1)))
 
-    for arrive in bulk:
-        arrive()
-
     def plane_weights(i):
         uy, uz = plane(vy, i + 1), plane(vz, i + 1)
         uyd = below_j(uy, edge_rows(vyl, 8 + i * CH))
@@ -620,8 +622,11 @@
         planes_of(te.at[t], 2, c1_o.at[t], 1, k_s, 1, t_r1.at[0, t], t_r1.at[1, t], 8, range(PLANES))
         return 0
 
-    lax.fori_loop(0, TR, own_planes, 0, unroll=2)
-    for arrive in got:
+    for chunk in range(CHUNKS):
+        for arrive in bulk[chunk]:
+            arrive()
+        lax.fori_loop(chunk * PER, (chunk + 1) * PER, own_planes, 0, unroll=2)
+    for arrive in late + got:
         arrive()
 
     for i, way in ((-1, (-1, 0)), (PLANES, (1, 0))):

time: 46.1 us -> 46.1 us (level)
  no operation moved by 1% of the time
where the time goes in v4:
time: 46.1 us
  Pallas kernels  45.4 us (98%)
  between operations  0.64 us (1%)
    pallas_call x1, Pallas kernels, body(): pl.pallas_call(pressure_kernel, out_shape=[shape(OWN, 128), shape(3, OWN,...  41.8 us
    pallas_call x1, Pallas kernels, body(): pl.pallas_call(transport_kernel, out_shape=[shape(OWN, 128), shape(3, OWN...  3.62 us

profile of v4, /device:TPU:1, one launch (start us, length us, event | category | flops | bytes accessed | tf_op | source)
XLA Modules:
  0.0 46.1 jit_solution(13801184659639301519)
XLA Ops:
  0.6 41.8 %shard_map.58 = (f32[512,128]{1,0:T(8,128)S(1)}, f32[3,512,128]{2,1,0:T(8,128)S(1)}, f32[7,512,128]{2,1,0:T(8,128)S(1)}, f32[16,576,128]{2,1,0:T(8,128)S(1)}, f32[2,16,64,128]{3,2,1,0:T(8,128)S(1)}) custom-call(f32[3,512,128]{2,1,0:T(8,128)} %bitcast.31, f32[3,512,128]{2,1,0:T(8,128)} %bitcast.32, f32[16,512,128]{2,1,0:T(8,128)} %bitcast.30), custom_call_target="tpu_custom_call" | custom-call | tf_op jit(solution)/shard_map/pallas_call | solution.py:712
  42.4 3.6 %shard_map.59 = (f32[512,128]{1,0:T(8,128)}, f32[3,512,128]{2,1,0:T(8,128)}, f32[16,512,128]{2,1,0:T(8,128)}) custom-call(f32[7,512,128]{2,1,0:T(8,128)S(1)} %get-tuple-element.11.k_ref, f32[16,576,128]{2,1,0:T(8,128)S(1)} %get-tuple-element.12.c1, f32[2,16,64,128]{3,2,1,0:T(8,128)S(1)} %get-tuple-element.13.c1n, f32[512,128]{1,0:T(8,128)S(1)} %get-tuple-element.14.p, ...), custom_call_target="tpu_custom_call" | custom-call | tf_op jit(solution)/shard_map/pallas_call | solution.py:739
